TPU v7x, 256 devices: a whole 4x4x8 slice. The times are simulated.
256 devices in a mesh: dp: 64 (over z, y, core), tensor: 4 (over x).
Axes of the slice: x: 4, y: 4, z: 8, core: 2. Of those that a mesh axis runs over, the one named last changes fastest.
Arguments:
- queries: bfloat16 [8192, 4096], P('dp', 'tensor'), may hold values from -6 to 6
- keys: bfloat16 [160, 1792, 512], P(None, ('dp', 'tensor')), may hold values from -4.375 to 4.375
- values: bfloat16 [160, 1792, 512], P(None, ('dp', 'tensor')), may hold values from -6 to 6
- d_out: bfloat16 [8192, 4096], P('dp', 'tensor'), may hold values from -6 to 6
- tile_sample: int32 [160], replicated, may hold values from 0 to 127, as said below
- row_sample: int32 [64, 128], P('dp'), may hold values from 0 to 1, never falling along the last dimension, each value on 1 to 96 neighbouring positions
Outputs:
- attn_out: bfloat16 [8192, 4096], P('dp', 'tensor')
- d_query: bfloat16 [8192, 4096], P('dp', 'tensor')
- d_key: bfloat16 [160, 1792, 512], P(None, ('dp', 'tensor'))
- d_value: bfloat16 [160, 1792, 512], P(None, ('dp', 'tensor'))
Inputs may be any that keep to these rules, and one draw needn't show every extreme that they name: `tile_sample`: every sample has one or two tiles; the samples of one text device have at most 3 tiles together, and some text device has exactly 3.
All inputs are finite; a program needn't handle non-finite values.
Results may differ from a plain program's by a relative error of at most 0.015.
Values may be sent and summed in bfloat16 or wider, within the bound.
No kernel may reach another device: no remote copies, remote signals or barrier semaphores. Data moves between devices by JAX's collectives and lax.ppermute only.
A program may use at most 192 MiB of HBM per device.

v0:
```python
import functools
import math

import jax
import jax.numpy as jnp
from jax import lax
from jax.experimental import pallas as pl
from jax.experimental.pallas import tpu as pltpu
from jax.sharding import Mesh
from jax.sharding import PartitionSpec as P

HD = 128
QH = 32
KVH = 4
PATCHES = 1601
SMP_DEV = 2
MAXT = 3
NZ = 8
NC = 8
ROWS = 128
HEADS = QH // KVH
RB = 4
RBR = ROWS // RB
BL = HEADS * RBR
LANES = HEADS * ROWS
SLOTS = NZ * MAXT
TOKS = 256
WIDE = (RB - 1) * BL
HALF = NZ // 2
NQ = ROWS + 16
NEG = -1e30
SCALE = 1.0 / math.sqrt(HD)
SCALE2 = SCALE / math.log(2.0)
BF = jnp.bfloat16
F32 = jnp.float32
MIB = 1024 * 1024


def dot(a, b, ca, cb):
    return lax.dot_general(a, b, (((ca,), (cb,)), ((), ())), preferred_element_type=F32)


def select_kernel(spot_ref, k_ref, v_ref, out_ref, rows_ref):
    spots = spot_ref.shape[0]
    tiles = k_ref.shape[0] // 7
    width = k_ref.shape[1]
    col = lax.broadcasted_iota(jnp.int32, (spots, tiles), 1)
    pick = jnp.where(col == spot_ref[...], 1.0, 0.0).astype(BF)
    for j, ref in enumerate((k_ref, v_ref)):
        for n in range(7):
            rows = dot(pick, ref[n * tiles : (n + 1) * tiles], 1, 0)
            for x in range(width // HD):
                rows_ref[j, x, pl.ds(n, spots, stride=8), :] = rows[:, x * HD : (x + 1) * HD]
        for x in range(width // HD):
            rows_ref[j, x, pl.ds(7, spots, stride=8), :] = jnp.zeros((spots, HD), F32)
            for c in range(NC):
                out_ref[c, x, j] = rows_ref[j, x, c * SLOTS * 8 : (c + 1) * SLOTS * 8].astype(BF)


def return_kernel(spot_ref, recv_ref, dk_ref, dv_ref, rows_ref):
    spots = NC * SLOTS
    tiles = spot_ref.shape[0]
    col = lax.broadcasted_iota(jnp.int32, (tiles, spots), 1)
    pick = jnp.where(col == spot_ref[...], 1.0, 0.0).astype(BF)
    for j in range(2):
        rows_ref[j] = recv_ref[:, 0, j].astype(F32).reshape(spots * 8, HD)
    for n in range(7):
        both = jnp.concatenate(
            [rows_ref[j, pl.ds(n, spots, stride=8), :].astype(BF) for j in range(2)], axis=1
        )
        rows = dot(pick, both, 1, 0).astype(BF)
        dk_ref[n * tiles : (n + 1) * tiles] = rows[:, :HD]
        dv_ref[n * tiles : (n + 1) * tiles] = rows[:, HD:]


def pack_kernel(row_ref, q_ref, do_ref, out_ref):
    first = jnp.sum(jnp.where(row_ref[...] == 0, 1.0, 0.0)).astype(jnp.int32)
    lane = lax.broadcasted_iota(jnp.int32, (16, LANES), 1)
    row = (lane // BL) * RBR + lane % RBR
    out_ref[:ROWS] = q_ref[...]
    out_ref[ROWS:NQ] = jnp.where(row >= first, 1.0, 0.0).astype(BF)
    out_ref[NQ:] = do_ref[...]


def load_rows(pack_ref, q_ref, do_ref, qt_ref, dot_ref):
    for rb in range(RB):
        sl = slice(rb * BL, (rb + 1) * BL)
        for h in range(HEADS):
            lo = rb * BL + h * RBR
            cols = slice(h * HD, (h + 1) * HD)
            q_ref[lo : lo + RBR] = pack_ref[0, rb * RBR : (rb + 1) * RBR, cols]
            do_ref[lo : lo + RBR] = pack_ref[0, NQ + rb * RBR : NQ + (rb + 1) * RBR, cols]
        qt_ref[0:HD, sl] = q_ref[sl].T
        dot_ref[:, sl] = do_ref[sl].T
    sample = pack_ref[0, ROWS:NQ, :]
    row = lax.broadcasted_iota(jnp.int32, (16, LANES), 0)
    off = jnp.where(
        row == 0, 1.0,
        jnp.where(
            ((row == 1) & (sample.astype(F32) > 0.5)) | ((row == 2) & (sample.astype(F32) < 0.5)),
            NEG, 0.0,
        ),
    )
    qt_ref[HD : HD + 16] = off.astype(BF)


def set_up(z, qt_ref, side_ref):
    qt_ref[HD:] = jnp.zeros((HD, LANES), BF)
    i = lax.broadcasted_iota(jnp.int32, (TOKS, HD), 0)
    lane = lax.broadcasted_iota(jnp.int32, (TOKS, HD), 1)
    n = i % 8
    pos = z * 224 + (i // 8) * 7 + n
    empty = (n >= 7) | (pos >= PATCHES)
    for j in range(SMP_DEV + 1):
        none = empty if j < SMP_DEV else lane >= 0
        side_ref[j] = jnp.where(
            lane == 0, jnp.where(none, NEG, 0.0), jnp.where(lane == 1 + j, 1.0, 0.0)
        ).astype(BF)


def slot_tokens(kv_ref, j, s):
    return kv_ref[:, j, s].reshape(TOKS, HD)


def stats_kernel(half, slot_ref, pack_ref, kv_ref, stat_ref,
                 q_ref, do_ref, qt_ref, dot_ref, side_ref, m_ref, l_ref, d_ref):
    here = pl.program_id(0)
    text = half * HALF + here

    @pl.when(here == 0)
    def _():
        set_up(slot_ref[0], qt_ref, side_ref)

    load_rows(pack_ref, q_ref, do_ref, qt_ref, dot_ref)
    m_ref[...] = jnp.full(m_ref.shape, 2 * NEG, F32)
    l_ref[...] = jnp.zeros(l_ref.shape, F32)
    d_ref[...] = jnp.zeros(d_ref.shape, F32)

    def slot(s):
        mark = slot_ref[1 + text * MAXT + s]
        owner = jnp.maximum(mark, 0)
        side = side_ref[jnp.where(mark < 0, SMP_DEV, owner)]
        k = jnp.concatenate([slot_tokens(kv_ref, 0, s), side], axis=1)
        v = slot_tokens(kv_ref, 1, s)
        sl = pl.ds(pl.multiple_of(owner * BL, BL), WIDE)
        sc = dot(k, qt_ref[:, sl], 1, 0)
        g = dot(v, dot_ref[:, sl], 1, 0)
        top = jnp.max(sc, axis=0, keepdims=True)
        p = jnp.exp2((sc - top) * SCALE2)
        total = jnp.sum(p, axis=0, keepdims=True)
        delta = jnp.sum(p * g, axis=0, keepdims=True)
        old = m_ref[:, sl]
        new = jnp.maximum(old, top)
        a = jnp.exp2((old - new) * SCALE2)
        b = jnp.exp2((top - new) * SCALE2)
        m_ref[:, sl] = new
        l_ref[:, sl] = l_ref[:, sl] * a + total * b
        d_ref[:, sl] = d_ref[:, sl] * a + delta * b

    for s in range(MAXT):
        slot(s)
    lse = m_ref[...] + jnp.log2(l_ref[...]) * (1.0 / SCALE2)
    delta = d_ref[...] / l_ref[...]
    for i in range(NZ):
        stat_ref[i, pl.ds(here, 1), :] = lse
        stat_ref[i, pl.ds(HALF + here, 1), :] = delta


def grad_kernel(half, slot_ref, pack_ref, kv_ref, stat_ref, *refs):
    (rows_ref, dkv_ref, q_ref, do_ref, qt_ref, dot_ref, side_ref,
     lse_ref, delta_ref, dq_ref, out_ref) = refs[2 * half :]
    here = pl.program_id(0)
    text = half * HALF + here

    @pl.when(here == 0)
    def _():
        set_up(slot_ref[0], qt_ref, side_ref)

    load_rows(pack_ref, q_ref, do_ref, qt_ref, dot_ref)
    lses = [stat_ref[i, pl.ds(here, 1), :] for i in range(NZ)]
    top = lses[0]
    for i in range(1, NZ):
        top = jnp.maximum(top, lses[i])
    weights = [jnp.exp2((v - top) * SCALE2) for v in lses]
    total = weights[0]
    delta = weights[0] * stat_ref[0, pl.ds(HALF + here, 1), :]
    for i in range(1, NZ):
        total = total + weights[i]
        delta = delta + weights[i] * stat_ref[i, pl.ds(HALF + here, 1), :]
    lse = top + jnp.log2(total) * (1.0 / SCALE2)
    lse_ref[...] = lse
    delta_ref[...] = delta / total
    out_ref[...] = jnp.zeros(out_ref.shape, F32)
    dq_ref[...] = jnp.zeros(dq_ref.shape, F32)

    def slot(s):
        mark = slot_ref[1 + text * MAXT + s]
        owner = jnp.maximum(mark, 0)
        side = side_ref[jnp.where(mark < 0, SMP_DEV, owner)]
        k = slot_tokens(kv_ref, 0, s)
        v = slot_tokens(kv_ref, 1, s)
        sl = pl.ds(pl.multiple_of(owner * BL, BL), WIDE)
        sc = dot(jnp.concatenate([k, side], axis=1), qt_ref[:, sl], 1, 0)
        g = dot(v, dot_ref[:, sl], 1, 0)
        p = jnp.exp2((sc - lse_ref[:, sl]) * SCALE2)
        ds = (p * (g - delta_ref[:, sl])).astype(BF)
        p = p.astype(BF)
        out_ref[:, sl] += dot(v.T, p, 1, 0)
        dq_ref[:, sl] += dot(k.T, ds, 1, 0)
        dk = dot(ds, q_ref[sl], 1, 0) * SCALE
        dv = dot(p, do_ref[sl], 1, 0)
        dkv_ref[:, 0, s] = dk.astype(BF).reshape(TOKS // 8, 8, HD)
        dkv_ref[:, 1, s] = dv.astype(BF).reshape(TOKS // 8, 8, HD)

    for s in range(MAXT):
        slot(s)
    rows_ref[0, 0] = out_ref[...].astype(BF)
    rows_ref[0, 1] = (dq_ref[...] * SCALE).astype(BF)


def turn_kernel(rows_ref, out_ref, dq_ref):
    for j, ref in enumerate((out_ref, dq_ref)):
        for rb in range(RB):
            turned = rows_ref[0, j, :, rb * BL : (rb + 1) * BL].astype(F32).T.astype(BF)
            for h in range(HEADS):
                ref[rb * RBR : (rb + 1) * RBR, h * HD : (h + 1) * HD] = turned[
                    h * RBR : (h + 1) * RBR
                ]


def params(mib):
    return pltpu.CompilerParams(vmem_limit_bytes=mib * MIB)


def per_device(queries, keys, values, d_out, tile_sample, row_sample):
    z = lax.axis_index("z")
    c = lax.axis_index("c")
    tiles, patch, width = keys.shape
    plane = ("c", "tensor")

    mine = pl.pallas_call(
        pack_kernel,
        out_shape=jax.ShapeDtypeStruct((NQ + ROWS, LANES), BF),
        compiler_params=params(56),
        name="pack",
    )(row_sample, queries, d_out)
    pack = lax.all_gather(mine, "z", axis=0, tiled=False)

    owner = tile_sample // SMP_DEV
    ids = jnp.arange(tiles, dtype=jnp.int32)
    rank = jnp.sum(
        ((owner[:, None] == owner[None, :]) & (ids[None, :] < ids[:, None])).astype(jnp.int32),
        axis=1, dtype=jnp.int32,
    )
    spot = (owner % NC) * SLOTS + (owner // NC) * MAXT + rank
    match = spot[None, :] == jnp.arange(NC * SLOTS, dtype=jnp.int32)[:, None]
    spot_tile = jnp.sum(jnp.where(match, ids[None, :] + 1, 0), axis=1, dtype=jnp.int32) - 1
    spot_sample = (
        jnp.sum(jnp.where(match, (tile_sample % SMP_DEV)[None, :] + 1, 0), axis=1, dtype=jnp.int32) - 1
    )
    slot_info = jnp.concatenate(
        [z.astype(jnp.int32)[None], lax.dynamic_slice_in_dim(spot_sample, c * SLOTS, SLOTS)]
    )

    flat = lambda a: a.transpose(1, 0, 2).reshape(patch * tiles, width)
    depth = patch * tiles
    spots = NC * SLOTS
    pair = 2 * HD
    sent = pl.pallas_call(
        select_kernel,
        grid=(width // pair,),
        in_specs=[
            pl.BlockSpec((spots, 1), lambda i: (0, 0)),
            pl.BlockSpec((depth, pair), lambda i: (0, i)),
            pl.BlockSpec((depth, pair), lambda i: (0, i)),
        ],
        out_specs=pl.BlockSpec((NC, 2, 2, SLOTS * 8, HD), lambda i: (0, i, 0, 0, 0)),
        out_shape=jax.ShapeDtypeStruct((NC, KVH, 2, SLOTS * 8, HD), BF),
        scratch_shapes=[pltpu.VMEM((2, pair // HD, spots * 8, HD), F32)],
        compiler_params=params(56),
        name="select",
    )(spot_tile[:, None], flat(keys), flat(values))
    kv = lax.all_to_all(
        sent.reshape(NC * KVH, 2 * SLOTS * 8, HD), plane, 0, 0, tiled=True
    ).reshape(NC * KVH, 2, SLOTS, 8, HD)

    row_scratch = [
        pltpu.VMEM((LANES, HD), BF),
        pltpu.VMEM((LANES, HD), BF),
        pltpu.VMEM((2 * HD, LANES), BF),
        pltpu.VMEM((HD, LANES), BF),
        pltpu.VMEM((SMP_DEV + 1, TOKS, HD), BF),
        pltpu.VMEM((1, LANES), F32),
        pltpu.VMEM((1, LANES), F32),
    ]
    whole = pl.BlockSpec(memory_space=pltpu.VMEM)
    pack_specs = [
        pl.BlockSpec((1, NQ + ROWS, LANES), lambda i, *_, h=h: (h * HALF + i, 0, 0))
        for h in range(2)
    ]
    kv_specs = [
        pl.BlockSpec((NC * KVH, 2, MAXT, 8, HD), lambda i, *_, h=h: (0, 0, h * HALF + i, 0, 0))
        for h in range(2)
    ]
    parts = []
    for h in range(2):
        stat = pl.pallas_call(
            functools.partial(stats_kernel, h),
            grid_spec=pltpu.PrefetchScalarGridSpec(
                num_scalar_prefetch=1,
                grid=(HALF,),
                in_specs=[pack_specs[h], kv_specs[h]],
                out_specs=pl.BlockSpec((NZ, NZ, LANES), lambda i, *_: (0, 0, 0)),
                scratch_shapes=row_scratch + [pltpu.VMEM((1, LANES), F32)],
            ),
            out_shape=jax.ShapeDtypeStruct((NZ, NZ, LANES), F32),
            compiler_params=params(56),
            name=f"stats{h}",
        )(slot_info, pack, kv)
        parts.append(lax.all_to_all(stat, "z", 0, 0, tiled=True))

    made = []
    for h in range(2):
        made = pl.pallas_call(
            functools.partial(grad_kernel, h),
            grid_spec=pltpu.PrefetchScalarGridSpec(
                num_scalar_prefetch=1,
                grid=(HALF,),
                in_specs=[pack_specs[h], kv_specs[h], whole]
                + [pl.BlockSpec(memory_space=pl.ANY)] * len(made),
                out_specs=[
                    pl.BlockSpec((1, 2, HD, LANES), lambda i, *_, h=h: (h * HALF + i, 0, 0, 0)),
                    kv_specs[h],
                ],
                scratch_shapes=row_scratch + [pltpu.VMEM((HD, LANES), F32)] * 2,
            ),
            out_shape=[
                jax.ShapeDtypeStruct((NZ, 2, HD, LANES), BF),
                jax.ShapeDtypeStruct((NC * KVH, 2, SLOTS, 8, HD), BF),
            ],
            input_output_aliases={4 + j: j for j in range(len(made))},
            compiler_params=params(56),
            name=f"grads{h}",
        )(slot_info, pack, kv, parts[h], *made)
    rows, dkv = made

    home = lax.psum_scatter(rows, "z", scatter_dimension=0, tiled=True)
    returned = lax.all_to_all(
        dkv.reshape(NC * KVH, 2 * SLOTS * 8, HD), plane, 0, 0, tiled=True
    ).reshape(NC, KVH, 2, SLOTS * 8, HD)

    d_key, d_value = pl.pallas_call(
        return_kernel,
        grid=(KVH,),
        in_specs=[
            pl.BlockSpec((tiles, 1), lambda i: (0, 0)),
            pl.BlockSpec((NC, 1, 2, SLOTS * 8, HD), lambda i: (0, i, 0, 0, 0)),
        ],
        out_specs=[pl.BlockSpec((depth, HD), lambda i: (0, i))] * 2,
        out_shape=[jax.ShapeDtypeStruct((depth, width), BF)] * 2,
        scratch_shapes=[pltpu.VMEM((2, spots * 8, HD), F32)],
        compiler_params=params(32),
        name="give_back",
    )(spot[:, None], returned)
    unflat = lambda a: a.reshape(patch, tiles, width).transpose(1, 0, 2)

    attn_out, d_query = pl.pallas_call(
        turn_kernel,
        out_shape=[jax.ShapeDtypeStruct((ROWS, LANES), BF)] * 2,
        compiler_params=params(56),
        name="turn",
    )(home)
    return (attn_out, d_query, unflat(d_key), unflat(d_value))


def solution(mesh):
    split = Mesh(mesh.devices.reshape(NZ, NC, KVH), ("z", "c", "tensor"))
    rows = P(("z", "c"), "tensor")
    tokens = P(None, ("z", "c", "tensor"), None)
    return jax.shard_map(
        per_device,
        mesh=split,
        in_specs=(rows, tokens, tokens, rows, P(), P(("z", "c"), None)),
        out_specs=(rows, rows, tokens, tokens),
        check_vma=False,
    )
```

profile of v0, /device:TPU:1, one launch (start us, length us, event | category | flops | bytes accessed | tf_op | source)
XLA Modules:
  0.0 188.7 jit_solution(10787302159949618698)
XLA Ops:
  7.2 0.0 all-gather.3.cloned.1.call-start
  7.2 2.0 %pack.1 = bf16[272,1024]{1,0:T(8,128)(2,1)} custom-call(s32[1,128]{1,0:T(1,128)} %row_ref.1, bf16[128,1024]{1,0:T(8,128)(2,1)} %q_ref.1, bf16[128,1024]{1,0:T(8,128)(2,1)} %do_ref.1), custom_call_target="tpu_custom_call" | custom-call | tf_op jit(solution)/shard_map/pack/pallas_call | solution.py:241
  9.2 0.0 all-gather.3.cloned.1.call-update
  9.2 0.7 fusion.4
  9.9 0.2 convert_reduce_fusion
  10.1 0.1 select_reduce_fusion
  10.3 0.8 copy.14.spot_ref
  11.1 4.4 %select.13 = bf16[8,4,2,192,128]{4,3,2,1,0:T(8,128)(2,1)} custom-call(s32[192,1]{1,0:T(8,128)} %copy.14.spot_ref, bf16[1120,512]{1,0:T(8,128)(2,1)} %bitcast.31, bf16[1120,512]{1,0:T(8,128)(2,1)} %bitcast.32), custom_call_target="tpu_custom_call" | custom-call | tf_op jit(solution)/shard_map/select/pallas_call | solution.py:269
  15.5 8.6 %all-to-all-start = ((bf16[32,384,128]{2,1,0:T(8,128)(2,1)}), bf16[32,384,128]{2,1,0:T(8,128)(2,1)S(1)}, u32[]{:S(2)}, u32[]{:S(2)}) async-start(bf16[32,384,128]{2,1,0:T(8,128)(2,1)} %bitcast.29), calls=%async_computation | async-start | bytes 6291456 | tf_op jit(solution)/shard_map/all_to_all | solution.py:283
  24.1 0.1 dynamic_slice.3
  24.2 0.6 pad_add_fusion.slot_ref
  24.8 37.3 %all-to-all-done = bf16[32,384,128]{2,1,0:T(8,128)(2,1)S(1)} async-done(((bf16[32,384,128]{2,1,0:T(8,128)(2,1)}), bf16[32,384,128]{2,1,0:T(8,128)(2,1)S(1)}, u32[]{:S(2)}, u32[]{:S(2)}) %all-to-all-start) | async-done | bytes 3145760 | tf_op jit(solution)/shard_map/all_to_all | solution.py:283
  62.0 0.0 copy-start
  62.0 9.4 %all-gather.3.cloned.1.call-done = bf16[2176,1024]{1,0:T(8,128)(2,1)} async-done(((bf16[272,1024]{1,0:T(8,128)(2,1)}), bf16[2176,1024]{1,0:T(8,128)(2,1)}) %all-gather.3.cloned.1.call-update) | async-done | bytes 4456464 | tf_op jit(solution)/shard_map/all_gather | solution.py:247
  71.5 0.0 copy-done
  71.5 7.7 %stats0.1 = f32[8,8,1024]{2,1,0:T(8,128)} custom-call(s32[25]{0:T(128)} %pad_add_fusion.slot_ref, bf16[8,272,1024]{2,1,0:T(8,128)(2,1)} %bitcast.25, bf16[32,2,24,8,128]{4,3,2,1,0:T(8,128)(2,1)} %bitcast.21), custom_call_target="tpu_custom_call" | custom-call | tf_op jit(solution)/shard_map/stats0/pallas_call | solution.py:307
  79.1 4.0 %all-to-all-start.2 = ((f32[8,8,1024]{2,1,0:T(8,128)}), f32[8,8,1024]{2,1,0:T(8,128)S(1)}, u32[]{:S(2)}, u32[]{:S(2)}) async-start(f32[8,8,1024]{2,1,0:T(8,128)} %stats0.1), calls=%async_computation.2 | async-start | bytes 524288 | tf_op jit(solution)/shard_map/all_to_all | solution.py:320
  83.2 7.7 %stats1.1 = f32[8,8,1024]{2,1,0:T(8,128)} custom-call(s32[25]{0:T(128)} %pad_add_fusion.slot_ref, bf16[8,272,1024]{2,1,0:T(8,128)(2,1)} %bitcast.26, bf16[32,2,24,8,128]{4,3,2,1,0:T(8,128)(2,1)} %bitcast.22), custom_call_target="tpu_custom_call" | custom-call | tf_op jit(solution)/shard_map/stats1/pallas_call | solution.py:307
  90.8 2.7 %all-to-all-done.2.stat_ref = f32[8,8,1024]{2,1,0:T(8,128)S(1)} async-done(((f32[8,8,1024]{2,1,0:T(8,128)}), f32[8,8,1024]{2,1,0:T(8,128)S(1)}, u32[]{:S(2)}, u32[]{:S(2)}) %all-to-all-start.2) | async-done | bytes 262176 | tf_op jit(solution)/shard_map/all_to_all | solution.py:320
  93.5 0.0 copy-start.2
  93.5 4.0 %all-to-all-start.1 = ((f32[8,8,1024]{2,1,0:T(8,128)}), f32[8,8,1024]{2,1,0:T(8,128)S(1)}, u32[]{:S(2)}, u32[]{:S(2)}) async-start(f32[8,8,1024]{2,1,0:T(8,128)} %stats1.1), calls=%async_computation.1 | async-start | bytes 524288 | tf_op jit(solution)/shard_map/all_to_all | solution.py:320
  97.5 0.0 reduce-scatter.2.cloned.1.call-start
  97.5 0.0 copy-done.2
  97.6 11.8 %grads0.1 = (bf16[8,2,128,1024]{3,2,1,0:T(8,128)(2,1)}, bf16[32,2,24,8,128]{4,3,2,1,0:T(8,128)(2,1)}) custom-call(s32[25]{0:T(128)} %pad_add_fusion.slot_ref, bf16[8,272,1024]{2,1,0:T(8,128)(2,1)} %bitcast.27, bf16[32,2,24,8,128]{4,3,2,1,0:T(8,128)(2,1)} %bitcast.23, f32[8,8,1024]{2,1,0:T(8,128)} %copy-done.2), custom_call_target="tpu_custom_call" | custom-call | tf_op jit(solution)/shard_map/grads0/pallas_call | solution.py:324
  109.3 0.0 all-to-all-done.1.stat_ref
  109.3 0.0 copy-start.1
  109.3 0.7 copy-done.1
  110.0 11.7 %grads1.1 = (bf16[8,2,128,1024]{3,2,1,0:T(8,128)(2,1)}, bf16[32,2,24,8,128]{4,3,2,1,0:T(8,128)(2,1)}) custom-call(s32[25]{0:T(128)} %pad_add_fusion.slot_ref, bf16[8,272,1024]{2,1,0:T(8,128)(2,1)} %bitcast.28, bf16[32,2,24,8,128]{4,3,2,1,0:T(8,128)(2,1)} %bitcast.24, f32[8,8,1024]{2,1,0:T(8,128)} %copy-done.1, ...), custom_call_target="tpu_custom_call", output_to_operand_aliasing={{0}: (4, {}), {1}: (5, {})} | custom-call | tf_op jit(solution)/shard_map/grads1/pallas_call | solution.py:324
  121.8 0.0 reduce-scatter.2.cloned.1.call-update
  121.8 8.8 %all-to-all-start.3 = ((bf16[32,384,128]{2,1,0:T(8,128)(2,1)}), bf16[32,384,128]{2,1,0:T(8,128)(2,1)S(1)}, u32[]{:S(2)}, u32[]{:S(2)}) async-start(bf16[32,384,128]{2,1,0:T(8,128)(2,1)} %bitcast.30), calls=%async_computation.4 | async-start | bytes 6291456 | tf_op jit(solution)/shard_map/all_to_all | solution.py:348
  130.6 0.1 copy.15.spot_ref
  130.7 37.8 %all-to-all-done.3 = bf16[32,384,128]{2,1,0:T(8,128)(2,1)S(1)} async-done(((bf16[32,384,128]{2,1,0:T(8,128)(2,1)}), bf16[32,384,128]{2,1,0:T(8,128)(2,1)S(1)}, u32[]{:S(2)}, u32[]{:S(2)}) %all-to-all-start.3) | async-done | bytes 3145760 | tf_op jit(solution)/shard_map/all_to_all | solution.py:348
  168.5 3.2 %give_back.1 = (bf16[1120,512]{1,0:T(8,128)(2,1)}, bf16[1120,512]{1,0:T(8,128)(2,1)}) custom-call(s32[160,1]{1,0:T(8,128)S(1)} %copy.15.spot_ref, bf16[8,4,2,192,128]{4,3,2,1,0:T(8,128)(2,1)S(1)} %bitcast.20), custom_call_target="tpu_custom_call" | custom-call | tf_op jit(solution)/shard_map/give_back/pallas_call | solution.py:352
  171.7 8.1 %reduce-scatter.2.cloned.1.call-done.rows_ref = bf16[1,2,128,1024]{3,2,1,0:T(8,128)(2,1)} async-done(((bf16[8,2,128,1024]{3,2,1,0:T(8,128)(2,1)}), bf16[1,2,128,1024]{3,2,1,0:T(8,128)(2,1)}) %reduce-scatter.2.cloned.1.call-update) | async-done | bytes 524304 | tf_op jit(solution)/shard_map/reduce_scatter | solution.py:347
  179.9 2.0 %turn.1 = (bf16[128,1024]{1,0:T(8,128)(2,1)}, bf16[128,1024]{1,0:T(8,128)(2,1)}) custom-call(bf16[1,2,128,1024]{3,2,1,0:T(8,128)(2,1)} %reduce-scatter.2.cloned.1.call-done.rows_ref), custom_call_target="tpu_custom_call" | custom-call | tf_op jit(solution)/shard_map/turn/pallas_call | solution.py:367
  (3 shorter events, 0.0 us)
Async XLA Ops:
  7.2 64.3 %all-gather.3.cloned.1.call-start = ((), (), s32[]{:S(2)}) async-start(), calls=%async_computation.6 | async-start | bytes 5013504 | tf_op jit(solution)/shard_map/all_gather | solution.py:247
  15.5 46.5 %all-to-all-start = ((bf16[32,384,128]{2,1,0:T(8,128)(2,1)}), bf16[32,384,128]{2,1,0:T(8,128)(2,1)S(1)}, u32[]{:S(2)}, u32[]{:S(2)}) async-start(bf16[32,384,128]{2,1,0:T(8,128)(2,1)} %bitcast.29), calls=%async_computation | async-start | bytes 6291456 | tf_op jit(solution)/shard_map/all_to_all | solution.py:283
  62.0 9.4 %copy-start = (bf16[32,384,128]{2,1,0:T(8,128)(2,1)}, bf16[32,384,128]{2,1,0:T(8,128)(2,1)S(1)}, u32[]{:S(2)}) copy-start(bf16[32,384,128]{2,1,0:T(8,128)(2,1)S(1)} %all-to-all-done) | copy-start | bytes 9437188
  79.1 14.4 %all-to-all-start.2 = ((f32[8,8,1024]{2,1,0:T(8,128)}), f32[8,8,1024]{2,1,0:T(8,128)S(1)}, u32[]{:S(2)}, u32[]{:S(2)}) async-start(f32[8,8,1024]{2,1,0:T(8,128)} %stats0.1), calls=%async_computation.2 | async-start | bytes 524288 | tf_op jit(solution)/shard_map/all_to_all | solution.py:320
  93.5 4.0 %copy-start.2 = (f32[8,8,1024]{2,1,0:T(8,128)}, f32[8,8,1024]{2,1,0:T(8,128)S(1)}, u32[]{:S(2)}) copy-start(f32[8,8,1024]{2,1,0:T(8,128)S(1)} %all-to-all-done.2.stat_ref) | copy-start | bytes 786436
  93.5 15.8 %all-to-all-start.1 = ((f32[8,8,1024]{2,1,0:T(8,128)}), f32[8,8,1024]{2,1,0:T(8,128)S(1)}, u32[]{:S(2)}, u32[]{:S(2)}) async-start(f32[8,8,1024]{2,1,0:T(8,128)} %stats1.1), calls=%async_computation.1 | async-start | bytes 524288 | tf_op jit(solution)/shard_map/all_to_all | solution.py:320
  97.5 82.4 %reduce-scatter.2.cloned.1.call-start = ((), (), s32[]{:S(2)}) async-start(), calls=%async_computation.5 | async-start | bytes 4718592 | tf_op jit(solution)/shard_map/reduce_scatter | solution.py:347
  109.3 0.7 copy-start.1
  121.8 46.7 %all-to-all-start.3 = ((bf16[32,384,128]{2,1,0:T(8,128)(2,1)}), bf16[32,384,128]{2,1,0:T(8,128)(2,1)S(1)}, u32[]{:S(2)}, u32[]{:S(2)}) async-start(bf16[32,384,128]{2,1,0:T(8,128)(2,1)} %bitcast.30), calls=%async_computation.4 | async-start | bytes 6291456 | tf_op jit(solution)/shard_map/all_to_all | solution.py:348
Sparse Core Ops, SparseCore 0:
  10.4 61.0 all-gather.2
  121.9 57.9 reduce-scatter.1
where the time goes:
time: 189 us
  waiting for transfers between devices  95.4 us (50%)
  Pallas kernels  50.5 us (27%)
  starting transfers between devices  25.4 us (13%)
  between operations  14.1 us (7%)
    all_to_all x1, waiting for transfers between devices, per_device(): lax.all_to_all(dkv.reshape(NC * KVH, 2 * SLOTS * 8, HD), plane, 0, 0, til...  37.8 us
    all_to_all x1, waiting for transfers between devices, per_device(): lax.all_to_all(sent.reshape(NC * KVH, 2 * SLOTS * 8, HD), plane, 0, 0, ti...  37.3 us
    pallas_call x2, Pallas kernels, per_device(): pl.pallas_call(functools.partial(grad_kernel, h), grid_spec=pltpu.Prefetc...  23.5 us
    pallas_call x2, Pallas kernels, per_device(): pl.pallas_call(functools.partial(stats_kernel, h), grid_spec=pltpu.Prefet...  15.3 us
    all_gather x1, waiting for transfers between devices, per_device(): pack = lax.all_gather(mine, 'z', axis=0, tiled=False)  9.44 us
    all_to_all x1, starting transfers between devices, per_device(): lax.all_to_all(dkv.reshape(NC * KVH, 2 * SLOTS * 8, HD), plane, 0, 0, til...  8.77 us
    all_to_all x1, starting transfers between devices, per_device(): lax.all_to_all(sent.reshape(NC * KVH, 2 * SLOTS * 8, HD), plane, 0, 0, ti...  8.59 us
    reduce_scatter x1, waiting for transfers between devices, per_device(): home = lax.psum_scatter(rows, 'z', scatter_dimension=0, tiled=True)  8.14 us
  transfers between devices with their start and end apart: 6, of which 5 were waited for; matrix products, arithmetic and copies ran while one was open for 1% of the time, Pallas kernels for 14%

commit v1 on v0

--- a/solution.py
+++ b/solution.py
@@ -27,7 +27,6 @@
 TOKS = 256
 WIDE = (RB - 1) * BL
 HALF = NZ // 2
-NQ = ROWS + 16
 NEG = -1e30
 SCALE = 1.0 / math.sqrt(HD)
 SCALE2 = SCALE / math.log(2.0)
@@ -73,33 +72,27 @@
         dv_ref[n * tiles : (n + 1) * tiles] = rows[:, HD:]
 
 
-def pack_kernel(row_ref, q_ref, do_ref, out_ref):
-    first = jnp.sum(jnp.where(row_ref[...] == 0, 1.0, 0.0)).astype(jnp.int32)
-    lane = lax.broadcasted_iota(jnp.int32, (16, LANES), 1)
-    row = (lane // BL) * RBR + lane % RBR
+def pack_kernel(q_ref, do_ref, out_ref):
     out_ref[:ROWS] = q_ref[...]
-    out_ref[ROWS:NQ] = jnp.where(row >= first, 1.0, 0.0).astype(BF)
-    out_ref[NQ:] = do_ref[...]
-
-
-def load_rows(pack_ref, q_ref, do_ref, qt_ref, dot_ref):
+    out_ref[ROWS:] = do_ref[...]
+
+
+def load_rows(first, pack_ref, q_ref, do_ref, qt_ref, dot_ref):
     for rb in range(RB):
         sl = slice(rb * BL, (rb + 1) * BL)
         for h in range(HEADS):
             lo = rb * BL + h * RBR
             cols = slice(h * HD, (h + 1) * HD)
             q_ref[lo : lo + RBR] = pack_ref[0, rb * RBR : (rb + 1) * RBR, cols]
-            do_ref[lo : lo + RBR] = pack_ref[0, NQ + rb * RBR : NQ + (rb + 1) * RBR, cols]
+            do_ref[lo : lo + RBR] = pack_ref[0, ROWS + rb * RBR : ROWS + (rb + 1) * RBR, cols]
         qt_ref[0:HD, sl] = q_ref[sl].T
         dot_ref[:, sl] = do_ref[sl].T
-    sample = pack_ref[0, ROWS:NQ, :]
+    lane = lax.broadcasted_iota(jnp.int32, (16, LANES), 1)
+    second = (lane // BL) * RBR + lane % RBR >= first
     row = lax.broadcasted_iota(jnp.int32, (16, LANES), 0)
     off = jnp.where(
         row == 0, 1.0,
-        jnp.where(
-            ((row == 1) & (sample.astype(F32) > 0.5)) | ((row == 2) & (sample.astype(F32) < 0.5)),
-            NEG, 0.0,
-        ),
+        jnp.where(((row == 1) & second) | ((row == 2) & ~second), NEG, 0.0),
     )
     qt_ref[HD : HD + 16] = off.astype(BF)
 
@@ -131,7 +124,7 @@
     def _():
         set_up(slot_ref[0], qt_ref, side_ref)
 
-    load_rows(pack_ref, q_ref, do_ref, qt_ref, dot_ref)
+    load_rows(slot_ref[1 + SLOTS + text], pack_ref, q_ref, do_ref, qt_ref, dot_ref)
     m_ref[...] = jnp.full(m_ref.shape, 2 * NEG, F32)
     l_ref[...] = jnp.zeros(l_ref.shape, F32)
     d_ref[...] = jnp.zeros(d_ref.shape, F32)
@@ -176,7 +169,7 @@
     def _():
         set_up(slot_ref[0], qt_ref, side_ref)
 
-    load_rows(pack_ref, q_ref, do_ref, qt_ref, dot_ref)
+    load_rows(slot_ref[1 + SLOTS + text], pack_ref, q_ref, do_ref, qt_ref, dot_ref)
     lses = [stat_ref[i, pl.ds(here, 1), :] for i in range(NZ)]
     top = lses[0]
     for i in range(1, NZ):
@@ -240,11 +233,24 @@
 
     mine = pl.pallas_call(
         pack_kernel,
-        out_shape=jax.ShapeDtypeStruct((NQ + ROWS, LANES), BF),
+        out_shape=jax.ShapeDtypeStruct((2 * ROWS, LANES), BF),
         compiler_params=params(56),
         name="pack",
-    )(row_sample, queries, d_out)
+    )(queries, d_out)
     pack = lax.all_gather(mine, "z", axis=0, tiled=False)
+
+    mine_first = jnp.sum(jnp.where(row_sample == 0, 1.0, 0.0), axis=1, keepdims=True)
+    mine_first = jnp.broadcast_to(mine_first, (1, HD))
+    firsts = [mine_first] + [
+        lax.ppermute(mine_first, "z", [(i, (i + by) % NZ) for i in range(NZ)])
+        for by in range(1, NZ)
+    ]
+    back = (z - jnp.arange(NZ, dtype=jnp.int32) + NZ) % NZ
+    firsts = jnp.concatenate(firsts, axis=0)[:, 0]
+    firsts = jnp.sum(
+        jnp.where(back[:, None] == jnp.arange(NZ, dtype=jnp.int32)[None, :], firsts[:, None], 0.0),
+        axis=0,
+    ).astype(jnp.int32)
 
     owner = tile_sample // SMP_DEV
     ids = jnp.arange(tiles, dtype=jnp.int32)
@@ -259,7 +265,7 @@
         jnp.sum(jnp.where(match, (tile_sample % SMP_DEV)[None, :] + 1, 0), axis=1, dtype=jnp.int32) - 1
     )
     slot_info = jnp.concatenate(
-        [z.astype(jnp.int32)[None], lax.dynamic_slice_in_dim(spot_sample, c * SLOTS, SLOTS)]
+        [z.astype(jnp.int32)[None], lax.dynamic_slice_in_dim(spot_sample, c * SLOTS, SLOTS), firsts]
     )
 
     flat = lambda a: a.transpose(1, 0, 2).reshape(patch * tiles, width)
@@ -295,7 +301,7 @@
     ]
     whole = pl.BlockSpec(memory_space=pltpu.VMEM)
     pack_specs = [
-        pl.BlockSpec((1, NQ + ROWS, LANES), lambda i, *_, h=h: (h * HALF + i, 0, 0))
+        pl.BlockSpec((1, 2 * ROWS, LANES), lambda i, *_, h=h: (h * HALF + i, 0, 0))
         for h in range(2)
     ]
     kv_specs = [

time: 189 us -> 187 us (0.989)
  waiting for transfers between devices: 95.4 us -> 74.8 us
  starting transfers between devices: 25.4 us -> 42.4 us
    all_to_all x1, waiting for transfers between devices: 37.3 us -> 17.2 us  [per_device(): lax.all_to_all(sent.reshape(NC * KVH, 2 * SLOTS * 8, HD), plane, 0, 0, ti...]
    ppermute x0 -> x7, starting transfers between devices: none -> 16.6 us  [per_device(): lax.ppermute(mine_first, 'z', [(i, (i + by) % NZ) for i in range(NZ)])]
    all_gather x1, waiting for transfers between devices: 9.44 us -> 7.13 us  [per_device(): pack = lax.all_gather(mine, 'z', axis=0, tiled=False)]
    ppermute x0 -> x7, waiting for transfers between devices: none -> 1.99 us  [per_device(): lax.ppermute(mine_first, 'z', [(i, (i + by) % NZ) for i in range(NZ)])]
  transfers between devices with their start and end apart: 6 -> 13, of which waited for: 5 -> 7; matrix products, arithmetic and copies ran while one was open for 1% -> 2% of each run, Pallas kernels for 14% -> 15%
where the time goes in v1:
time: 187 us; the launch traced here: 186 us
  waiting for transfers between devices  74.8 us (40%)
  Pallas kernels  50.3 us (27%)
  starting transfers between devices  42.4 us (23%)
  between operations  14.1 us (8%)
  local copies, waits for them, and re-layouts  2.45 us (1%)
  other arithmetic  2.35 us (1%)
    all_to_all x1, waiting for transfers between devices, per_device(): lax.all_to_all(dkv.reshape(NC * KVH, 2 * SLOTS * 8, HD), plane, 0, 0, til...  37.8 us
    pallas_call x2, Pallas kernels, per_device(): pl.pallas_call(functools.partial(grad_kernel, h), grid_spec=pltpu.Prefetc...  23.5 us
    all_to_all x1, waiting for transfers between devices, per_device(): lax.all_to_all(sent.reshape(NC * KVH, 2 * SLOTS * 8, HD), plane, 0, 0, ti...  17.2 us
    ppermute x7, starting transfers between devices, per_device(): lax.ppermute(mine_first, 'z', [(i, (i + by) % NZ) for i in range(NZ)])  16.6 us
    pallas_call x2, Pallas kernels, per_device(): pl.pallas_call(functools.partial(stats_kernel, h), grid_spec=pltpu.Prefet...  15.3 us
    all_to_all x1, starting transfers between devices, per_device(): lax.all_to_all(dkv.reshape(NC * KVH, 2 * SLOTS * 8, HD), plane, 0, 0, til...  8.82 us
    all_to_all x1, starting transfers between devices, per_device(): lax.all_to_all(sent.reshape(NC * KVH, 2 * SLOTS * 8, HD), plane, 0, 0, ti...  8.73 us
    all_to_all x2, starting transfers between devices, per_device(): parts.append(lax.all_to_all(stat, 'z', 0, 0, tiled=True))  8 us
  transfers between devices with their start and end apart: 13, of which 7 were waited for; matrix products, arithmetic and copies ran while one was open for 2% of the time, Pallas kernels for 15%

profile of v1, /device:TPU:1, one launch (start us, length us, event | category | flops | bytes accessed | tf_op | source)
XLA Modules:
  0.0 186.4 jit_solution(10019317320581877724)
XLA Ops:
  7.2 0.0 all-gather.3.cloned.1.call-start
  7.2 1.9 pack.1
  9.1 0.0 all-gather.3.cloned.1.call-update
  9.1 0.7 fusion.4
  9.8 0.2 convert_reduce_fusion
  10.0 0.1 select_reduce_fusion
  10.2 0.8 copy.18.spot_ref
  10.9 4.4 %select.21 = bf16[8,4,2,192,128]{4,3,2,1,0:T(8,128)(2,1)} custom-call(s32[192,1]{1,0:T(8,128)} %copy.18.spot_ref, bf16[1120,512]{1,0:T(8,128)(2,1)} %bitcast.31, bf16[1120,512]{1,0:T(8,128)(2,1)} %bitcast.32), custom_call_target="tpu_custom_call" | custom-call | tf_op jit(solution)/shard_map/select/pallas_call | solution.py:275
  15.3 8.7 %all-to-all-start = ((bf16[32,384,128]{2,1,0:T(8,128)(2,1)}), bf16[32,384,128]{2,1,0:T(8,128)(2,1)S(1)}, u32[]{:S(2)}, u32[]{:S(2)}) async-start(bf16[32,384,128]{2,1,0:T(8,128)(2,1)} %bitcast.29), calls=%async_computation | async-start | bytes 6291456 | tf_op jit(solution)/shard_map/all_to_all | solution.py:289
  24.0 0.6 fusion.5
  24.6 0.6 broadcast_in_dim.68
  25.3 1.7 collective-permute-start
  27.0 3.0 %collective-permute-start.1 = (f32[1,128]{1,0:T(1,128)S(1)}, f32[1,128]{1,0:T(1,128)S(1)}, u32[]{:S(2)}, u32[]{:S(2)}) collective-permute-start(f32[1,128]{1,0:T(1,128)S(1)} %broadcast_in_dim.68), channel_id=1, source_target_pairs={{0,64},{32,96},{64,128},{96,160},{128,192},{160,224},{192,0},{224,... | collective-permute-start | bytes 1544 | tf_op jit(solution)/shard_map/ppermute | solution.py:245
  30.0 3.7 %collective-permute-start.2 = (f32[1,128]{1,0:T(1,128)S(1)}, f32[1,128]{1,0:T(1,128)S(1)}, u32[]{:S(2)}, u32[]{:S(2)}) collective-permute-start(f32[1,128]{1,0:T(1,128)S(1)} %broadcast_in_dim.68), channel_id=1, source_target_pairs={{0,96},{32,128},{64,160},{96,192},{128,224},{160,0},{192,32},{224,... | collective-permute-start | bytes 1544 | tf_op jit(solution)/shard_map/ppermute | solution.py:245
  33.8 0.5 collective-permute-start.3
  34.2 4.5 %collective-permute-start.4 = (f32[1,128]{1,0:T(1,128)S(1)}, f32[1,128]{1,0:T(1,128)S(1)}, u32[]{:S(2)}, u32[]{:S(2)}) collective-permute-start(f32[1,128]{1,0:T(1,128)S(1)} %broadcast_in_dim.68), channel_id=1, source_target_pairs={{0,160},{32,192},{64,224},{96,0},{128,32},{160,64},{192,96},{224,1... | collective-permute-start | bytes 1544 | tf_op jit(solution)/shard_map/ppermute | solution.py:245
  38.7 0.0 collective-permute-done
  38.7 2.5 %collective-permute-start.5 = (f32[1,128]{1,0:T(1,128)S(1)}, f32[1,128]{1,0:T(1,128)S(1)}, u32[]{:S(2)}, u32[]{:S(2)}) collective-permute-start(f32[1,128]{1,0:T(1,128)S(1)} %broadcast_in_dim.68), channel_id=1, source_target_pairs={{0,192},{32,224},{64,0},{96,32},{128,64},{160,96},{192,128},{224,1... | collective-permute-start | bytes 1544 | tf_op jit(solution)/shard_map/ppermute | solution.py:245
  41.2 0.0 collective-permute-done.1
  41.2 0.7 collective-permute-start.6
  41.9 0.1 dynamic_slice.3
  42.0 0.0 collective-permute-done.2
  42.0 0.0 collective-permute-done.3
  42.0 0.0 collective-permute-done.4
  42.0 0.5 collective-permute-done.5
  42.5 1.5 collective-permute-done.6
  44.0 0.1 slice_reduce_fusion
  44.1 0.1 select_reduce_fusion.2
  44.2 0.6 pad_add_fusion.slot_ref
  44.8 17.2 %all-to-all-done = bf16[32,384,128]{2,1,0:T(8,128)(2,1)S(1)} async-done(((bf16[32,384,128]{2,1,0:T(8,128)(2,1)}), bf16[32,384,128]{2,1,0:T(8,128)(2,1)S(1)}, u32[]{:S(2)}, u32[]{:S(2)}) %all-to-all-start) | async-done | bytes 3145760 | tf_op jit(solution)/shard_map/all_to_all | solution.py:289
  62.0 7.1 %all-gather.3.cloned.1.call-done = bf16[2048,1024]{1,0:T(8,128)(2,1)} async-done(((bf16[256,1024]{1,0:T(8,128)(2,1)}), bf16[2048,1024]{1,0:T(8,128)(2,1)}) %all-gather.3.cloned.1.call-update) | async-done | bytes 4194320 | tf_op jit(solution)/shard_map/all_gather | solution.py:240
  69.1 7.6 %stats0.1 = f32[8,8,1024]{2,1,0:T(8,128)} custom-call(s32[33]{0:T(128)} %pad_add_fusion.slot_ref, bf16[8,256,1024]{2,1,0:T(8,128)(2,1)} %bitcast.25, bf16[32,2,24,8,128]{4,3,2,1,0:T(8,128)(2,1)} %bitcast.21), custom_call_target="tpu_custom_call" | custom-call | tf_op jit(solution)/shard_map/stats0/pallas_call | solution.py:313
  76.7 4.0 %all-to-all-start.2 = ((f32[8,8,1024]{2,1,0:T(8,128)}), f32[8,8,1024]{2,1,0:T(8,128)S(1)}, u32[]{:S(2)}, u32[]{:S(2)}) async-start(f32[8,8,1024]{2,1,0:T(8,128)} %stats0.1), calls=%async_computation.2 | async-start | bytes 524288 | tf_op jit(solution)/shard_map/all_to_all | solution.py:326
  80.8 7.6 %stats1.1 = f32[8,8,1024]{2,1,0:T(8,128)} custom-call(s32[33]{0:T(128)} %pad_add_fusion.slot_ref, bf16[8,256,1024]{2,1,0:T(8,128)(2,1)} %bitcast.26, bf16[32,2,24,8,128]{4,3,2,1,0:T(8,128)(2,1)} %bitcast.22), custom_call_target="tpu_custom_call" | custom-call | tf_op jit(solution)/shard_map/stats1/pallas_call | solution.py:313
  88.4 2.7 %all-to-all-done.2.stat_ref = f32[8,8,1024]{2,1,0:T(8,128)S(1)} async-done(((f32[8,8,1024]{2,1,0:T(8,128)}), f32[8,8,1024]{2,1,0:T(8,128)S(1)}, u32[]{:S(2)}, u32[]{:S(2)}) %all-to-all-start.2) | async-done | bytes 262176 | tf_op jit(solution)/shard_map/all_to_all | solution.py:326
  91.1 4.0 %all-to-all-start.1 = ((f32[8,8,1024]{2,1,0:T(8,128)}), f32[8,8,1024]{2,1,0:T(8,128)S(1)}, u32[]{:S(2)}, u32[]{:S(2)}) async-start(f32[8,8,1024]{2,1,0:T(8,128)} %stats1.1), calls=%async_computation.1 | async-start | bytes 524288 | tf_op jit(solution)/shard_map/all_to_all | solution.py:326
  95.1 0.2 reduce-scatter.2.cloned.1.call-start
  95.3 11.8 %grads0.1 = (bf16[8,2,128,1024]{3,2,1,0:T(8,128)(2,1)}, bf16[32,2,24,8,128]{4,3,2,1,0:T(8,128)(2,1)}) custom-call(s32[33]{0:T(128)} %pad_add_fusion.slot_ref, bf16[8,256,1024]{2,1,0:T(8,128)(2,1)} %bitcast.27, bf16[32,2,24,8,128]{4,3,2,1,0:T(8,128)(2,1)} %bitcast.23, f32[8,8,1024]{2,1,0:T(8,128)} %copy-done.2), custom_call_target="tpu_custom_call" | custom-call | tf_op jit(solution)/shard_map/grads0/pallas_call | solution.py:330
  107.1 0.0 all-to-all-done.1.stat_ref
  107.1 0.7 copy-done.1
  107.8 11.8 %grads1.1 = (bf16[8,2,128,1024]{3,2,1,0:T(8,128)(2,1)}, bf16[32,2,24,8,128]{4,3,2,1,0:T(8,128)(2,1)}) custom-call(s32[33]{0:T(128)} %pad_add_fusion.slot_ref, bf16[8,256,1024]{2,1,0:T(8,128)(2,1)} %bitcast.28, bf16[32,2,24,8,128]{4,3,2,1,0:T(8,128)(2,1)} %bitcast.24, f32[8,8,1024]{2,1,0:T(8,128)} %copy-done.1, ...), custom_call_target="tpu_custom_call", output_to_operand_aliasing={{0}: (4, {}), {1}: (5, {})} | custom-call | tf_op jit(solution)/shard_map/grads1/pallas_call | solution.py:330
  119.6 0.0 reduce-scatter.2.cloned.1.call-update
  119.6 8.8 %all-to-all-start.3 = ((bf16[32,384,128]{2,1,0:T(8,128)(2,1)}), bf16[32,384,128]{2,1,0:T(8,128)(2,1)S(1)}, u32[]{:S(2)}, u32[]{:S(2)}) async-start(bf16[32,384,128]{2,1,0:T(8,128)(2,1)} %bitcast.30), calls=%async_computation.4 | async-start | bytes 6291456 | tf_op jit(solution)/shard_map/all_to_all | solution.py:354
  128.4 0.1 copy.19.spot_ref
  128.5 37.8 %all-to-all-done.3 = bf16[32,384,128]{2,1,0:T(8,128)(2,1)S(1)} async-done(((bf16[32,384,128]{2,1,0:T(8,128)(2,1)}), bf16[32,384,128]{2,1,0:T(8,128)(2,1)S(1)}, u32[]{:S(2)}, u32[]{:S(2)}) %all-to-all-start.3) | async-done | bytes 3145760 | tf_op jit(solution)/shard_map/all_to_all | solution.py:354
  166.4 3.2 %give_back.1 = (bf16[1120,512]{1,0:T(8,128)(2,1)}, bf16[1120,512]{1,0:T(8,128)(2,1)}) custom-call(s32[160,1]{1,0:T(8,128)S(1)} %copy.19.spot_ref, bf16[8,4,2,192,128]{4,3,2,1,0:T(8,128)(2,1)S(1)} %bitcast.20), custom_call_target="tpu_custom_call" | custom-call | tf_op jit(solution)/shard_map/give_back/pallas_call | solution.py:358
  169.6 7.9 %reduce-scatter.2.cloned.1.call-done.rows_ref = bf16[1,2,128,1024]{3,2,1,0:T(8,128)(2,1)} async-done(((bf16[8,2,128,1024]{3,2,1,0:T(8,128)(2,1)}), bf16[1,2,128,1024]{3,2,1,0:T(8,128)(2,1)}) %reduce-scatter.2.cloned.1.call-update) | async-done | bytes 524304 | tf_op jit(solution)/shard_map/reduce_scatter | solution.py:353
  177.6 2.0 %turn.1 = (bf16[128,1024]{1,0:T(8,128)(2,1)}, bf16[128,1024]{1,0:T(8,128)(2,1)}) custom-call(bf16[1,2,128,1024]{3,2,1,0:T(8,128)(2,1)} %reduce-scatter.2.cloned.1.call-done.rows_ref), custom_call_target="tpu_custom_call" | custom-call | tf_op jit(solution)/shard_map/turn/pallas_call | solution.py:373
  (13 shorter events, 0.1 us)
Async XLA Ops:
  7.2 61.9 %all-gather.3.cloned.1.call-start = ((), (), s32[]{:S(2)}) async-start(), calls=%async_computation.6 | async-start | bytes 4718592 | tf_op jit(solution)/shard_map/all_gather | solution.py:240
  15.3 8.7 %copy-start.3 = (s32[1,128]{1,0:T(1,128)S(1)}, s32[1,128]{1,0:T(1,128)}, u32[]{:S(2)}) copy-start(s32[1,128]{1,0:T(1,128)} %param.11) | copy-start | bytes 1540
  15.3 46.7 %all-to-all-start = ((bf16[32,384,128]{2,1,0:T(8,128)(2,1)}), bf16[32,384,128]{2,1,0:T(8,128)(2,1)S(1)}, u32[]{:S(2)}, u32[]{:S(2)}) async-start(bf16[32,384,128]{2,1,0:T(8,128)(2,1)} %bitcast.29), calls=%async_computation | async-start | bytes 6291456 | tf_op jit(solution)/shard_map/all_to_all | solution.py:289
  25.3 13.4 %collective-permute-start = (f32[1,128]{1,0:T(1,128)S(1)}, f32[1,128]{1,0:T(1,128)S(1)}, u32[]{:S(2)}, u32[]{:S(2)}) collective-permute-start(f32[1,128]{1,0:T(1,128)S(1)} %broadcast_in_dim.68), channel_id=1, source_target_pairs={{0,32},{32,64},{64,96},{96,128},{128,160},{160,192},{192,224},{224... | collective-permute-start | bytes 1544 | tf_op jit(solution)/shard_map/ppermute | solution.py:245
  27.0 14.2 %collective-permute-start.1 = (f32[1,128]{1,0:T(1,128)S(1)}, f32[1,128]{1,0:T(1,128)S(1)}, u32[]{:S(2)}, u32[]{:S(2)}) collective-permute-start(f32[1,128]{1,0:T(1,128)S(1)} %broadcast_in_dim.68), channel_id=1, source_target_pairs={{0,64},{32,96},{64,128},{96,160},{128,192},{160,224},{192,0},{224,... | collective-permute-start | bytes 1544 | tf_op jit(solution)/shard_map/ppermute | solution.py:245
  30.0 12.0 %collective-permute-start.2 = (f32[1,128]{1,0:T(1,128)S(1)}, f32[1,128]{1,0:T(1,128)S(1)}, u32[]{:S(2)}, u32[]{:S(2)}) collective-permute-start(f32[1,128]{1,0:T(1,128)S(1)} %broadcast_in_dim.68), channel_id=1, source_target_pairs={{0,96},{32,128},{64,160},{96,192},{128,224},{160,0},{192,32},{224,... | collective-permute-start | bytes 1544 | tf_op jit(solution)/shard_map/ppermute | solution.py:245
  33.8 8.2 %collective-permute-start.3 = (f32[1,128]{1,0:T(1,128)S(1)}, f32[1,128]{1,0:T(1,128)S(1)}, u32[]{:S(2)}, u32[]{:S(2)}) collective-permute-start(f32[1,128]{1,0:T(1,128)S(1)} %broadcast_in_dim.68), channel_id=1, source_target_pairs={{0,128},{32,160},{64,192},{96,224},{128,0},{160,32},{192,64},{224,... | collective-permute-start | bytes 1544 | tf_op jit(solution)/shard_map/ppermute | solution.py:245
  34.2 7.8 %collective-permute-start.4 = (f32[1,128]{1,0:T(1,128)S(1)}, f32[1,128]{1,0:T(1,128)S(1)}, u32[]{:S(2)}, u32[]{:S(2)}) collective-permute-start(f32[1,128]{1,0:T(1,128)S(1)} %broadcast_in_dim.68), channel_id=1, source_target_pairs={{0,160},{32,192},{64,224},{96,0},{128,32},{160,64},{192,96},{224,1... | collective-permute-start | bytes 1544 | tf_op jit(solution)/shard_map/ppermute | solution.py:245
  38.7 3.8 %collective-permute-start.5 = (f32[1,128]{1,0:T(1,128)S(1)}, f32[1,128]{1,0:T(1,128)S(1)}, u32[]{:S(2)}, u32[]{:S(2)}) collective-permute-start(f32[1,128]{1,0:T(1,128)S(1)} %broadcast_in_dim.68), channel_id=1, source_target_pairs={{0,192},{32,224},{64,0},{96,32},{128,64},{160,96},{192,128},{224,1... | collective-permute-start | bytes 1544 | tf_op jit(solution)/shard_map/ppermute | solution.py:245
  41.2 2.8 %collective-permute-start.6 = (f32[1,128]{1,0:T(1,128)S(1)}, f32[1,128]{1,0:T(1,128)S(1)}, u32[]{:S(2)}, u32[]{:S(2)}) collective-permute-start(f32[1,128]{1,0:T(1,128)S(1)} %broadcast_in_dim.68), channel_id=1, source_target_pairs={{0,224},{32,0},{64,32},{96,64},{128,96},{160,128},{192,160},{224,1... | collective-permute-start | bytes 1544 | tf_op jit(solution)/shard_map/ppermute | solution.py:245
  62.0 7.1 %copy-start = (bf16[32,384,128]{2,1,0:T(8,128)(2,1)}, bf16[32,384,128]{2,1,0:T(8,128)(2,1)S(1)}, u32[]{:S(2)}) copy-start(bf16[32,384,128]{2,1,0:T(8,128)(2,1)S(1)} %all-to-all-done) | copy-start | bytes 9437188
  76.7 14.4 %all-to-all-start.2 = ((f32[8,8,1024]{2,1,0:T(8,128)}), f32[8,8,1024]{2,1,0:T(8,128)S(1)}, u32[]{:S(2)}, u32[]{:S(2)}) async-start(f32[8,8,1024]{2,1,0:T(8,128)} %stats0.1), calls=%async_computation.2 | async-start | bytes 524288 | tf_op jit(solution)/shard_map/all_to_all | solution.py:326
  91.1 4.2 %copy-start.2 = (f32[8,8,1024]{2,1,0:T(8,128)}, f32[8,8,1024]{2,1,0:T(8,128)S(1)}, u32[]{:S(2)}) copy-start(f32[8,8,1024]{2,1,0:T(8,128)S(1)} %all-to-all-done.2.stat_ref) | copy-start | bytes 786436
  91.1 16.0 %all-to-all-start.1 = ((f32[8,8,1024]{2,1,0:T(8,128)}), f32[8,8,1024]{2,1,0:T(8,128)S(1)}, u32[]{:S(2)}, u32[]{:S(2)}) async-start(f32[8,8,1024]{2,1,0:T(8,128)} %stats1.1), calls=%async_computation.1 | async-start | bytes 524288 | tf_op jit(solution)/shard_map/all_to_all | solution.py:326
  95.1 82.5 %reduce-scatter.2.cloned.1.call-start = ((), (), s32[]{:S(2)}) async-start(), calls=%async_computation.5 | async-start | bytes 4718592 | tf_op jit(solution)/shard_map/reduce_scatter | solution.py:353
  107.1 0.7 copy-start.1
  119.6 46.8 %all-to-all-start.3 = ((bf16[32,384,128]{2,1,0:T(8,128)(2,1)}), bf16[32,384,128]{2,1,0:T(8,128)(2,1)S(1)}, u32[]{:S(2)}, u32[]{:S(2)}) async-start(bf16[32,384,128]{2,1,0:T(8,128)(2,1)} %bitcast.30), calls=%async_computation.4 | async-start | bytes 6291456 | tf_op jit(solution)/shard_map/all_to_all | solution.py:354
Sparse Core Ops, SparseCore 0:
  10.4 58.6 all-gather.2
  119.7 57.7 reduce-scatter.1

commit v2 on v1

--- a/solution.py
+++ b/solution.py
@@ -159,27 +159,30 @@
         stat_ref[i, pl.ds(HALF + here, 1), :] = delta
 
 
-def grad_kernel(half, slot_ref, pack_ref, kv_ref, stat_ref, *refs):
-    (rows_ref, dkv_ref, q_ref, do_ref, qt_ref, dot_ref, side_ref,
-     lse_ref, delta_ref, dq_ref, out_ref) = refs[2 * half :]
+def grad_kernel(half, base, keep, aliased, slot_ref, pack_ref, kv_ref, stat_ref, *refs):
+    refs = refs[aliased:]
+    rows_ref = refs[0] if base == 0 else None
+    dkv_ref = refs[1] if base == 0 else refs[0]
+    (q_ref, do_ref, qt_ref, dot_ref, side_ref,
+     lse_ref, delta_ref, dq_ref, out_ref, ds_ref, p_ref) = refs[-11:]
     here = pl.program_id(0)
-    text = half * HALF + here
+    text = half * HALF + base + here
 
     @pl.when(here == 0)
     def _():
         set_up(slot_ref[0], qt_ref, side_ref)
 
     load_rows(slot_ref[1 + SLOTS + text], pack_ref, q_ref, do_ref, qt_ref, dot_ref)
-    lses = [stat_ref[i, pl.ds(here, 1), :] for i in range(NZ)]
+    lses = [stat_ref[i, pl.ds(base + here, 1), :] for i in range(NZ)]
     top = lses[0]
     for i in range(1, NZ):
         top = jnp.maximum(top, lses[i])
     weights = [jnp.exp2((v - top) * SCALE2) for v in lses]
     total = weights[0]
-    delta = weights[0] * stat_ref[0, pl.ds(HALF + here, 1), :]
+    delta = weights[0] * stat_ref[0, pl.ds(HALF + base + here, 1), :]
     for i in range(1, NZ):
         total = total + weights[i]
-        delta = delta + weights[i] * stat_ref[i, pl.ds(HALF + here, 1), :]
+        delta = delta + weights[i] * stat_ref[i, pl.ds(HALF + base + here, 1), :]
     lse = top + jnp.log2(total) * (1.0 / SCALE2)
     lse_ref[...] = lse
     delta_ref[...] = delta / total
@@ -198,8 +201,16 @@
         p = jnp.exp2((sc - lse_ref[:, sl]) * SCALE2)
         ds = (p * (g - delta_ref[:, sl])).astype(BF)
         p = p.astype(BF)
-        out_ref[:, sl] += dot(v.T, p, 1, 0)
-        dq_ref[:, sl] += dot(k.T, ds, 1, 0)
+        if rows_ref is not None:
+            out_ref[:, sl] += dot(v.T, p, 1, 0)
+            dq_ref[:, sl] += dot(k.T, ds, 1, 0)
+        if keep is None:
+            tokens(s, sl, ds, p)
+        else:
+            ds_ref[s] = ds
+            p_ref[s] = p
+
+    def tokens(s, sl, ds, p):
         dk = dot(ds, q_ref[sl], 1, 0) * SCALE
         dv = dot(p, do_ref[sl], 1, 0)
         dkv_ref[:, 0, s] = dk.astype(BF).reshape(TOKS // 8, 8, HD)
@@ -207,8 +218,17 @@
 
     for s in range(MAXT):
         slot(s)
-    rows_ref[0, 0] = out_ref[...].astype(BF)
-    rows_ref[0, 1] = (dq_ref[...] * SCALE).astype(BF)
+    if rows_ref is not None:
+        rows_ref[0, 0] = out_ref[...].astype(BF)
+        rows_ref[0, 1] = (dq_ref[...] * SCALE).astype(BF)
+    if keep is not None:
+
+        @pl.when(here < keep)
+        def _():
+            for s in range(MAXT):
+                owner = jnp.maximum(slot_ref[1 + text * MAXT + s], 0)
+                sl = pl.ds(pl.multiple_of(owner * BL, BL), WIDE)
+                tokens(s, sl, ds_ref[s], p_ref[s])
 
 
 def turn_kernel(rows_ref, out_ref, dq_ref):
@@ -325,31 +345,42 @@
         )(slot_info, pack, kv)
         parts.append(lax.all_to_all(stat, "z", 0, 0, tiled=True))
 
-    made = []
-    for h in range(2):
-        made = pl.pallas_call(
-            functools.partial(grad_kernel, h),
+    rows_shape = jax.ShapeDtypeStruct((NZ, 2, HD, LANES), BF)
+    dkv_shape = jax.ShapeDtypeStruct((NC * KVH, 2, SLOTS, 8, HD), BF)
+
+    def grads(h, base, keep, made):
+        first = h * HALF + base
+        last = HALF - 1 if keep is None else keep - 1
+        kv_block = (NC * KVH, 2, MAXT, 8, HD)
+        rows_out = pl.BlockSpec((1, 2, HD, LANES), lambda i, *_: (first + i, 0, 0, 0))
+        dkv_out = pl.BlockSpec(
+            kv_block, lambda i, *_: (0, 0, first + jnp.minimum(i, last), 0, 0)
+        )
+        return pl.pallas_call(
+            functools.partial(grad_kernel, h, base, keep, len(made)),
             grid_spec=pltpu.PrefetchScalarGridSpec(
                 num_scalar_prefetch=1,
-                grid=(HALF,),
-                in_specs=[pack_specs[h], kv_specs[h], whole]
+                grid=(HALF - base,),
+                in_specs=[
+                    pl.BlockSpec((1, 2 * ROWS, LANES), lambda i, *_: (first + i, 0, 0)),
+                    pl.BlockSpec(kv_block, lambda i, *_: (0, 0, first + i, 0, 0)),
+                    pl.BlockSpec((NZ, NZ, LANES), lambda i, *_: (0, 0, 0)),
+                ]
                 + [pl.BlockSpec(memory_space=pl.ANY)] * len(made),
-                out_specs=[
-                    pl.BlockSpec((1, 2, HD, LANES), lambda i, *_, h=h: (h * HALF + i, 0, 0, 0)),
-                    kv_specs[h],
-                ],
-                scratch_shapes=row_scratch + [pltpu.VMEM((HD, LANES), F32)] * 2,
+                out_specs=[rows_out, dkv_out] if base == 0 else [dkv_out],
+                scratch_shapes=row_scratch
+                + [pltpu.VMEM((HD, LANES), F32)] * 2
+                + [pltpu.VMEM((MAXT, TOKS, WIDE), BF)] * 2,
             ),
-            out_shape=[
-                jax.ShapeDtypeStruct((NZ, 2, HD, LANES), BF),
-                jax.ShapeDtypeStruct((NC * KVH, 2, SLOTS, 8, HD), BF),
-            ],
+            out_shape=[rows_shape, dkv_shape] if base == 0 else [dkv_shape],
             input_output_aliases={4 + j: j for j in range(len(made))},
             compiler_params=params(56),
-            name=f"grads{h}",
+            name=f"grads{h}{base}",
         )(slot_info, pack, kv, parts[h], *made)
-    rows, dkv = made
-
+
+    made = grads(0, 0, None, ())
+    rows, dkv = grads(1, 0, HALF // 2, made)
+    (dkv,) = grads(1, HALF // 2, None, (dkv,))
     home = lax.psum_scatter(rows, "z", scatter_dimension=0, tiled=True)
     returned = lax.all_to_all(
         dkv.reshape(NC * KVH, 2 * SLOTS * 8, HD), plane, 0, 0, tiled=True

time: 187 us -> 187 us (level)
  waiting for transfers between devices: 74.8 us -> 68.7 us
  Pallas kernels: 50.3 us -> 55.8 us
    reduce_scatter x1, waiting for transfers between devices: 7.95 us -> 1.85 us  [per_device(): home = lax.psum_scatter(rows, 'z', scatter_dimension=0, tiled=True)]
    pallas_call x2 -> x3, Pallas kernels: 23.5 us -> 29.1 us  [grads(): pl.pallas_call(functools.partial(grad_kernel, h, base, keep, len(made)),...]
  transfers between devices with their start and end apart: 13 -> 13, of which waited for: 7 -> 7; matrix products, arithmetic and copies ran while one was open for 2% -> 2% of each run, Pallas kernels for 15% -> 18%
where the time goes in v2:
time: 187 us; the launch traced here: 186 us
  waiting for transfers between devices  68.7 us (37%)
  Pallas kernels  55.8 us (30%)
  starting transfers between devices  42.4 us (23%)
  between operations  14.1 us (8%)
  local copies, waits for them, and re-layouts  2.45 us (1%)
  other arithmetic  2.35 us (1%)
    all_to_all x1, waiting for transfers between devices, per_device(): lax.all_to_all(dkv.reshape(NC * KVH, 2 * SLOTS * 8, HD), plane, 0, 0, til...  37.8 us
    pallas_call x3, Pallas kernels, grads(): pl.pallas_call(functools.partial(grad_kernel, h, base, keep, len(made)),...  29.1 us
    all_to_all x1, waiting for transfers between devices, per_device(): lax.all_to_all(sent.reshape(NC * KVH, 2 * SLOTS * 8, HD), plane, 0, 0, ti...  17.2 us
    ppermute x7, starting transfers between devices, per_device(): lax.ppermute(mine_first, 'z', [(i, (i + by) % NZ) for i in range(NZ)])  16.6 us
    pallas_call x2, Pallas kernels, per_device(): pl.pallas_call(functools.partial(stats_kernel, h), grid_spec=pltpu.Prefet...  15.3 us
    all_to_all x1, starting transfers between devices, per_device(): lax.all_to_all(dkv.reshape(NC * KVH, 2 * SLOTS * 8, HD), plane, 0, 0, til...  8.83 us
    all_to_all x1, starting transfers between devices, per_device(): lax.all_to_all(sent.reshape(NC * KVH, 2 * SLOTS * 8, HD), plane, 0, 0, ti...  8.73 us
    all_to_all x2, starting transfers between devices, per_device(): parts.append(lax.all_to_all(stat, 'z', 0, 0, tiled=True))  8 us
  transfers between devices with their start and end apart: 13, of which 7 were waited for; matrix products, arithmetic and copies ran while one was open for 2% of the time, Pallas kernels for 18%

profile of v2, /device:TPU:1, one launch (start us, length us, event | category | flops | bytes accessed | tf_op | source)
XLA Modules:
  0.0 185.8 jit_solution(18133816437404886707)
XLA Ops:
  7.2 0.0 all-gather.3.cloned.1.call-start
  7.2 1.9 pack.1
  9.1 0.0 all-gather.3.cloned.1.call-update
  9.1 0.7 fusion.4
  9.8 0.2 convert_reduce_fusion
  10.0 0.1 select_reduce_fusion
  10.2 0.8 copy.19.spot_ref
  10.9 4.4 %select.21 = bf16[8,4,2,192,128]{4,3,2,1,0:T(8,128)(2,1)} custom-call(s32[192,1]{1,0:T(8,128)} %copy.19.spot_ref, bf16[1120,512]{1,0:T(8,128)(2,1)} %bitcast.33, bf16[1120,512]{1,0:T(8,128)(2,1)} %bitcast.34), custom_call_target="tpu_custom_call" | custom-call | tf_op jit(solution)/shard_map/select/pallas_call | solution.py:295
  15.3 8.7 %all-to-all-start = ((bf16[32,384,128]{2,1,0:T(8,128)(2,1)}), bf16[32,384,128]{2,1,0:T(8,128)(2,1)S(1)}, u32[]{:S(2)}, u32[]{:S(2)}) async-start(bf16[32,384,128]{2,1,0:T(8,128)(2,1)} %bitcast.32), calls=%async_computation | async-start | bytes 6291456 | tf_op jit(solution)/shard_map/all_to_all | solution.py:309
  24.0 0.6 fusion.5
  24.6 0.6 broadcast_in_dim.68
  25.3 1.7 collective-permute-start
  27.0 3.0 %collective-permute-start.1 = (f32[1,128]{1,0:T(1,128)S(1)}, f32[1,128]{1,0:T(1,128)S(1)}, u32[]{:S(2)}, u32[]{:S(2)}) collective-permute-start(f32[1,128]{1,0:T(1,128)S(1)} %broadcast_in_dim.68), channel_id=1, source_target_pairs={{0,64},{32,96},{64,128},{96,160},{128,192},{160,224},{192,0},{224,... | collective-permute-start | bytes 1544 | tf_op jit(solution)/shard_map/ppermute | solution.py:265
  30.0 3.7 %collective-permute-start.2 = (f32[1,128]{1,0:T(1,128)S(1)}, f32[1,128]{1,0:T(1,128)S(1)}, u32[]{:S(2)}, u32[]{:S(2)}) collective-permute-start(f32[1,128]{1,0:T(1,128)S(1)} %broadcast_in_dim.68), channel_id=1, source_target_pairs={{0,96},{32,128},{64,160},{96,192},{128,224},{160,0},{192,32},{224,... | collective-permute-start | bytes 1544 | tf_op jit(solution)/shard_map/ppermute | solution.py:265
  33.8 0.5 collective-permute-start.3
  34.2 4.5 %collective-permute-start.4 = (f32[1,128]{1,0:T(1,128)S(1)}, f32[1,128]{1,0:T(1,128)S(1)}, u32[]{:S(2)}, u32[]{:S(2)}) collective-permute-start(f32[1,128]{1,0:T(1,128)S(1)} %broadcast_in_dim.68), channel_id=1, source_target_pairs={{0,160},{32,192},{64,224},{96,0},{128,32},{160,64},{192,96},{224,1... | collective-permute-start | bytes 1544 | tf_op jit(solution)/shard_map/ppermute | solution.py:265
  38.7 0.0 collective-permute-done
  38.7 2.5 %collective-permute-start.5 = (f32[1,128]{1,0:T(1,128)S(1)}, f32[1,128]{1,0:T(1,128)S(1)}, u32[]{:S(2)}, u32[]{:S(2)}) collective-permute-start(f32[1,128]{1,0:T(1,128)S(1)} %broadcast_in_dim.68), channel_id=1, source_target_pairs={{0,192},{32,224},{64,0},{96,32},{128,64},{160,96},{192,128},{224,1... | collective-permute-start | bytes 1544 | tf_op jit(solution)/shard_map/ppermute | solution.py:265
  41.2 0.0 collective-permute-done.1
  41.2 0.7 collective-permute-start.6
  41.9 0.1 dynamic_slice.3
  42.0 0.0 collective-permute-done.2
  42.0 0.0 collective-permute-done.3
  42.0 0.0 collective-permute-done.4
  42.0 0.5 collective-permute-done.5
  42.5 1.5 collective-permute-done.6
  44.0 0.1 slice_reduce_fusion
  44.1 0.1 select_reduce_fusion.2
  44.2 0.6 pad_add_fusion.slot_ref
  44.8 17.2 %all-to-all-done = bf16[32,384,128]{2,1,0:T(8,128)(2,1)S(1)} async-done(((bf16[32,384,128]{2,1,0:T(8,128)(2,1)}), bf16[32,384,128]{2,1,0:T(8,128)(2,1)S(1)}, u32[]{:S(2)}, u32[]{:S(2)}) %all-to-all-start) | async-done | bytes 3145760 | tf_op jit(solution)/shard_map/all_to_all | solution.py:309
  62.0 7.1 %all-gather.3.cloned.1.call-done = bf16[2048,1024]{1,0:T(8,128)(2,1)} async-done(((bf16[256,1024]{1,0:T(8,128)(2,1)}), bf16[2048,1024]{1,0:T(8,128)(2,1)}) %all-gather.3.cloned.1.call-update) | async-done | bytes 4194320 | tf_op jit(solution)/shard_map/all_gather | solution.py:260
  69.1 7.6 %stats0.1 = f32[8,8,1024]{2,1,0:T(8,128)} custom-call(s32[33]{0:T(128)} %pad_add_fusion.slot_ref, bf16[8,256,1024]{2,1,0:T(8,128)(2,1)} %bitcast.26, bf16[32,2,24,8,128]{4,3,2,1,0:T(8,128)(2,1)} %bitcast.21), custom_call_target="tpu_custom_call" | custom-call | tf_op jit(solution)/shard_map/stats0/pallas_call | solution.py:333
  76.8 4.0 %all-to-all-start.2 = ((f32[8,8,1024]{2,1,0:T(8,128)}), f32[8,8,1024]{2,1,0:T(8,128)S(1)}, u32[]{:S(2)}, u32[]{:S(2)}) async-start(f32[8,8,1024]{2,1,0:T(8,128)} %stats0.1), calls=%async_computation.2 | async-start | bytes 524288 | tf_op jit(solution)/shard_map/all_to_all | solution.py:346
  80.8 7.6 %stats1.1 = f32[8,8,1024]{2,1,0:T(8,128)} custom-call(s32[33]{0:T(128)} %pad_add_fusion.slot_ref, bf16[8,256,1024]{2,1,0:T(8,128)(2,1)} %bitcast.27, bf16[32,2,24,8,128]{4,3,2,1,0:T(8,128)(2,1)} %bitcast.22), custom_call_target="tpu_custom_call" | custom-call | tf_op jit(solution)/shard_map/stats1/pallas_call | solution.py:333
  88.4 2.7 %all-to-all-done.2.stat_ref = f32[8,8,1024]{2,1,0:T(8,128)S(1)} async-done(((f32[8,8,1024]{2,1,0:T(8,128)}), f32[8,8,1024]{2,1,0:T(8,128)S(1)}, u32[]{:S(2)}, u32[]{:S(2)}) %all-to-all-start.2) | async-done | bytes 262176 | tf_op jit(solution)/shard_map/all_to_all | solution.py:346
  91.1 4.0 %all-to-all-start.1 = ((f32[8,8,1024]{2,1,0:T(8,128)}), f32[8,8,1024]{2,1,0:T(8,128)S(1)}, u32[]{:S(2)}, u32[]{:S(2)}) async-start(f32[8,8,1024]{2,1,0:T(8,128)} %stats1.1), calls=%async_computation.1 | async-start | bytes 524288 | tf_op jit(solution)/shard_map/all_to_all | solution.py:346
  95.1 0.2 reduce-scatter.2.cloned.1.call-start
  95.3 11.8 %grads00.1 = (bf16[8,2,128,1024]{3,2,1,0:T(8,128)(2,1)}, bf16[32,2,24,8,128]{4,3,2,1,0:T(8,128)(2,1)}) custom-call(s32[33]{0:T(128)} %pad_add_fusion.slot_ref, bf16[8,256,1024]{2,1,0:T(8,128)(2,1)} %bitcast.28, bf16[32,2,24,8,128]{4,3,2,1,0:T(8,128)(2,1)} %bitcast.23, f32[8,8,1024]{2,1,0:T(8,128)} %copy-done.2), custom_call_target="tpu_custom_call" | custom-call | tf_op jit(solution)/shard_map/grads00/pallas_call | solution.py:359
  107.2 0.7 copy-done.1
  107.9 11.1 %grads10.1 = (bf16[8,2,128,1024]{3,2,1,0:T(8,128)(2,1)}, bf16[32,2,24,8,128]{4,3,2,1,0:T(8,128)(2,1)}) custom-call(s32[33]{0:T(128)} %pad_add_fusion.slot_ref, bf16[8,256,1024]{2,1,0:T(8,128)(2,1)} %bitcast.29, bf16[32,2,24,8,128]{4,3,2,1,0:T(8,128)(2,1)} %bitcast.24, f32[8,8,1024]{2,1,0:T(8,128)} %copy-done.1, ...), custom_call_target="tpu_custom_call", output_to_operand_aliasing={{0}: (4, {}), {1}: (5, {})} | custom-call | tf_op jit(solution)/shard_map/grads10/pallas_call | solution.py:359
  119.0 0.0 reduce-scatter.2.cloned.1.call-update
  119.0 6.1 %grads12.1 = bf16[32,2,24,8,128]{4,3,2,1,0:T(8,128)(2,1)} custom-call(s32[33]{0:T(128)} %pad_add_fusion.slot_ref, bf16[8,256,1024]{2,1,0:T(8,128)(2,1)} %bitcast.30, bf16[32,2,24,8,128]{4,3,2,1,0:T(8,128)(2,1)} %bitcast.25, f32[8,8,1024]{2,1,0:T(8,128)} %copy-done.1, ...), custom_call_target="tpu_custom_call", output_to_operand_aliasing={{}: (4, {})} | custom-call | tf_op jit(solution)/shard_map/grads12/pallas_call | solution.py:359
  125.1 8.8 %all-to-all-start.3 = ((bf16[32,384,128]{2,1,0:T(8,128)(2,1)}), bf16[32,384,128]{2,1,0:T(8,128)(2,1)S(1)}, u32[]{:S(2)}, u32[]{:S(2)}) async-start(bf16[32,384,128]{2,1,0:T(8,128)(2,1)} %bitcast.31), calls=%async_computation.4 | async-start | bytes 6291456 | tf_op jit(solution)/shard_map/all_to_all | solution.py:385
  134.0 0.1 copy.20.spot_ref
  134.1 37.8 %all-to-all-done.3 = bf16[32,384,128]{2,1,0:T(8,128)(2,1)S(1)} async-done(((bf16[32,384,128]{2,1,0:T(8,128)(2,1)}), bf16[32,384,128]{2,1,0:T(8,128)(2,1)S(1)}, u32[]{:S(2)}, u32[]{:S(2)}) %all-to-all-start.3) | async-done | bytes 3145760 | tf_op jit(solution)/shard_map/all_to_all | solution.py:385
  171.9 3.2 %give_back.1 = (bf16[1120,512]{1,0:T(8,128)(2,1)}, bf16[1120,512]{1,0:T(8,128)(2,1)}) custom-call(s32[160,1]{1,0:T(8,128)S(1)} %copy.20.spot_ref, bf16[8,4,2,192,128]{4,3,2,1,0:T(8,128)(2,1)S(1)} %bitcast.20), custom_call_target="tpu_custom_call" | custom-call | tf_op jit(solution)/shard_map/give_back/pallas_call | solution.py:389
  175.2 1.8 reduce-scatter.2.cloned.1.call-done.rows_ref
  177.0 2.0 %turn.1 = (bf16[128,1024]{1,0:T(8,128)(2,1)}, bf16[128,1024]{1,0:T(8,128)(2,1)}) custom-call(bf16[1,2,128,1024]{3,2,1,0:T(8,128)(2,1)} %reduce-scatter.2.cloned.1.call-done.rows_ref), custom_call_target="tpu_custom_call" | custom-call | tf_op jit(solution)/shard_map/turn/pallas_call | solution.py:404
  (14 shorter events, 0.1 us)
Async XLA Ops:
  7.2 61.9 %all-gather.3.cloned.1.call-start = ((), (), s32[]{:S(2)}) async-start(), calls=%async_computation.6 | async-start | bytes 4718592 | tf_op jit(solution)/shard_map/all_gather | solution.py:260
  15.3 8.7 %copy-start.3 = (s32[1,128]{1,0:T(1,128)S(1)}, s32[1,128]{1,0:T(1,128)}, u32[]{:S(2)}) copy-start(s32[1,128]{1,0:T(1,128)} %param.11) | copy-start | bytes 1540
  15.3 46.7 %all-to-all-start = ((bf16[32,384,128]{2,1,0:T(8,128)(2,1)}), bf16[32,384,128]{2,1,0:T(8,128)(2,1)S(1)}, u32[]{:S(2)}, u32[]{:S(2)}) async-start(bf16[32,384,128]{2,1,0:T(8,128)(2,1)} %bitcast.32), calls=%async_computation | async-start | bytes 6291456 | tf_op jit(solution)/shard_map/all_to_all | solution.py:309
  25.3 13.4 %collective-permute-start = (f32[1,128]{1,0:T(1,128)S(1)}, f32[1,128]{1,0:T(1,128)S(1)}, u32[]{:S(2)}, u32[]{:S(2)}) collective-permute-start(f32[1,128]{1,0:T(1,128)S(1)} %broadcast_in_dim.68), channel_id=1, source_target_pairs={{0,32},{32,64},{64,96},{96,128},{128,160},{160,192},{192,224},{224... | collective-permute-start | bytes 1544 | tf_op jit(solution)/shard_map/ppermute | solution.py:265
  27.0 14.2 %collective-permute-start.1 = (f32[1,128]{1,0:T(1,128)S(1)}, f32[1,128]{1,0:T(1,128)S(1)}, u32[]{:S(2)}, u32[]{:S(2)}) collective-permute-start(f32[1,128]{1,0:T(1,128)S(1)} %broadcast_in_dim.68), channel_id=1, source_target_pairs={{0,64},{32,96},{64,128},{96,160},{128,192},{160,224},{192,0},{224,... | collective-permute-start | bytes 1544 | tf_op jit(solution)/shard_map/ppermute | solution.py:265
  30.0 12.0 %collective-permute-start.2 = (f32[1,128]{1,0:T(1,128)S(1)}, f32[1,128]{1,0:T(1,128)S(1)}, u32[]{:S(2)}, u32[]{:S(2)}) collective-permute-start(f32[1,128]{1,0:T(1,128)S(1)} %broadcast_in_dim.68), channel_id=1, source_target_pairs={{0,96},{32,128},{64,160},{96,192},{128,224},{160,0},{192,32},{224,... | collective-permute-start | bytes 1544 | tf_op jit(solution)/shard_map/ppermute | solution.py:265
  33.8 8.2 %collective-permute-start.3 = (f32[1,128]{1,0:T(1,128)S(1)}, f32[1,128]{1,0:T(1,128)S(1)}, u32[]{:S(2)}, u32[]{:S(2)}) collective-permute-start(f32[1,128]{1,0:T(1,128)S(1)} %broadcast_in_dim.68), channel_id=1, source_target_pairs={{0,128},{32,160},{64,192},{96,224},{128,0},{160,32},{192,64},{224,... | collective-permute-start | bytes 1544 | tf_op jit(solution)/shard_map/ppermute | solution.py:265
  34.2 7.8 %collective-permute-start.4 = (f32[1,128]{1,0:T(1,128)S(1)}, f32[1,128]{1,0:T(1,128)S(1)}, u32[]{:S(2)}, u32[]{:S(2)}) collective-permute-start(f32[1,128]{1,0:T(1,128)S(1)} %broadcast_in_dim.68), channel_id=1, source_target_pairs={{0,160},{32,192},{64,224},{96,0},{128,32},{160,64},{192,96},{224,1... | collective-permute-start | bytes 1544 | tf_op jit(solution)/shard_map/ppermute | solution.py:265
  38.7 3.8 %collective-permute-start.5 = (f32[1,128]{1,0:T(1,128)S(1)}, f32[1,128]{1,0:T(1,128)S(1)}, u32[]{:S(2)}, u32[]{:S(2)}) collective-permute-start(f32[1,128]{1,0:T(1,128)S(1)} %broadcast_in_dim.68), channel_id=1, source_target_pairs={{0,192},{32,224},{64,0},{96,32},{128,64},{160,96},{192,128},{224,1... | collective-permute-start | bytes 1544 | tf_op jit(solution)/shard_map/ppermute | solution.py:265
  41.2 2.8 %collective-permute-start.6 = (f32[1,128]{1,0:T(1,128)S(1)}, f32[1,128]{1,0:T(1,128)S(1)}, u32[]{:S(2)}, u32[]{:S(2)}) collective-permute-start(f32[1,128]{1,0:T(1,128)S(1)} %broadcast_in_dim.68), channel_id=1, source_target_pairs={{0,224},{32,0},{64,32},{96,64},{128,96},{160,128},{192,160},{224,1... | collective-permute-start | bytes 1544 | tf_op jit(solution)/shard_map/ppermute | solution.py:265
  62.0 7.1 %copy-start = (bf16[32,384,128]{2,1,0:T(8,128)(2,1)}, bf16[32,384,128]{2,1,0:T(8,128)(2,1)S(1)}, u32[]{:S(2)}) copy-start(bf16[32,384,128]{2,1,0:T(8,128)(2,1)S(1)} %all-to-all-done) | copy-start | bytes 9437188
  76.8 14.4 %all-to-all-start.2 = ((f32[8,8,1024]{2,1,0:T(8,128)}), f32[8,8,1024]{2,1,0:T(8,128)S(1)}, u32[]{:S(2)}, u32[]{:S(2)}) async-start(f32[8,8,1024]{2,1,0:T(8,128)} %stats0.1), calls=%async_computation.2 | async-start | bytes 524288 | tf_op jit(solution)/shard_map/all_to_all | solution.py:346
  91.1 4.2 %copy-start.2 = (f32[8,8,1024]{2,1,0:T(8,128)}, f32[8,8,1024]{2,1,0:T(8,128)S(1)}, u32[]{:S(2)}) copy-start(f32[8,8,1024]{2,1,0:T(8,128)S(1)} %all-to-all-done.2.stat_ref) | copy-start | bytes 786436
  91.1 16.0 %all-to-all-start.1 = ((f32[8,8,1024]{2,1,0:T(8,128)}), f32[8,8,1024]{2,1,0:T(8,128)S(1)}, u32[]{:S(2)}, u32[]{:S(2)}) async-start(f32[8,8,1024]{2,1,0:T(8,128)} %stats1.1), calls=%async_computation.1 | async-start | bytes 524288 | tf_op jit(solution)/shard_map/all_to_all | solution.py:346
  95.1 81.9 %reduce-scatter.2.cloned.1.call-start = ((), (), s32[]{:S(2)}) async-start(), calls=%async_computation.5 | async-start | bytes 4718592 | tf_op jit(solution)/shard_map/reduce_scatter | solution.py:384
  107.2 0.7 copy-start.1
  125.1 46.8 %all-to-all-start.3 = ((bf16[32,384,128]{2,1,0:T(8,128)(2,1)}), bf16[32,384,128]{2,1,0:T(8,128)(2,1)S(1)}, u32[]{:S(2)}, u32[]{:S(2)}) async-start(bf16[32,384,128]{2,1,0:T(8,128)(2,1)} %bitcast.31), calls=%async_computation.4 | async-start | bytes 6291456 | tf_op jit(solution)/shard_map/all_to_all | solution.py:385
Sparse Core Ops, SparseCore 0:
  10.4 58.6 all-gather.2
  119.1 57.8 reduce-scatter.1

commit v3 on v2

--- a/solution.py
+++ b/solution.py
@@ -73,8 +73,13 @@
 
 
 def pack_kernel(q_ref, do_ref, out_ref):
-    out_ref[:ROWS] = q_ref[...]
-    out_ref[ROWS:] = do_ref[...]
+    @pl.when(pl.program_id(0) == 0)
+    def _():
+        out_ref[...] = q_ref[...]
+
+    @pl.when(pl.program_id(0) == 1)
+    def _():
+        out_ref[...] = do_ref[...]
 
 
 def load_rows(first, pack_ref, q_ref, do_ref, qt_ref, dot_ref):
@@ -253,6 +258,9 @@
 
     mine = pl.pallas_call(
         pack_kernel,
+        grid=(2,),
+        in_specs=[pl.BlockSpec((ROWS, LANES), lambda i: (0, 0))] * 2,
+        out_specs=pl.BlockSpec((ROWS, LANES), lambda i: (i, 0)),
         out_shape=jax.ShapeDtypeStruct((2 * ROWS, LANES), BF),
         compiler_params=params(56),
         name="pack",

time: 187 us -> 187 us (level)
  no operation moved by 1% of the time
where the time goes in v3:
time: 187 us; the launch traced here: 186 us
  waiting for transfers between devices  68.7 us (37%)
  Pallas kernels  55.8 us (30%)
  starting transfers between devices  42.4 us (23%)
  between operations  14.1 us (8%)
  local copies, waits for them, and re-layouts  2.45 us (1%)
  other arithmetic  2.35 us (1%)
    all_to_all x1, waiting for transfers between devices, per_device(): lax.all_to_all(dkv.reshape(NC * KVH, 2 * SLOTS * 8, HD), plane, 0, 0, til...  37.8 us
    pallas_call x3, Pallas kernels, grads(): pl.pallas_call(functools.partial(grad_kernel, h, base, keep, len(made)),...  29.1 us
    all_to_all x1, waiting for transfers between devices, per_device(): lax.all_to_all(sent.reshape(NC * KVH, 2 * SLOTS * 8, HD), plane, 0, 0, ti...  17.2 us
    ppermute x7, starting transfers between devices, per_device(): lax.ppermute(mine_first, 'z', [(i, (i + by) % NZ) for i in range(NZ)])  16.6 us
    pallas_call x2, Pallas kernels, per_device(): pl.pallas_call(functools.partial(stats_kernel, h), grid_spec=pltpu.Prefet...  15.3 us
    all_to_all x1, starting transfers between devices, per_device(): lax.all_to_all(dkv.reshape(NC * KVH, 2 * SLOTS * 8, HD), plane, 0, 0, til...  8.82 us
    all_to_all x1, starting transfers between devices, per_device(): lax.all_to_all(sent.reshape(NC * KVH, 2 * SLOTS * 8, HD), plane, 0, 0, ti...  8.72 us
    all_to_all x2, starting transfers between devices, per_device(): parts.append(lax.all_to_all(stat, 'z', 0, 0, tiled=True))  7.99 us
  transfers between devices with their start and end apart: 13, of which 7 were waited for; matrix products, arithmetic and copies ran while one was open for 2% of the time, Pallas kernels for 18%

profile of v3, /device:TPU:1, one launch (start us, length us, event | category | flops | bytes accessed | tf_op | source)
XLA Modules:
  0.0 185.8 jit_solution(6085336065082592405)
XLA Ops:
  7.2 0.0 all-gather.3.cloned.1.call-start
  7.2 1.9 %pack.1 = bf16[256,1024]{1,0:T(8,128)(2,1)} custom-call(bf16[128,1024]{1,0:T(8,128)(2,1)} %q_ref.1, bf16[128,1024]{1,0:T(8,128)(2,1)} %do_ref.1), custom_call_target="tpu_custom_call" | custom-call | tf_op jit(solution)/shard_map/pack/pallas_call | solution.py:259
  9.1 0.0 all-gather.3.cloned.1.call-update
  9.1 0.7 fusion.4
  9.8 0.2 convert_reduce_fusion
  10.0 0.1 select_reduce_fusion
  10.2 0.8 copy.19.spot_ref
  10.9 4.4 %select.21 = bf16[8,4,2,192,128]{4,3,2,1,0:T(8,128)(2,1)} custom-call(s32[192,1]{1,0:T(8,128)} %copy.19.spot_ref, bf16[1120,512]{1,0:T(8,128)(2,1)} %bitcast.33, bf16[1120,512]{1,0:T(8,128)(2,1)} %bitcast.34), custom_call_target="tpu_custom_call" | custom-call | tf_op jit(solution)/shard_map/select/pallas_call | solution.py:303
  15.3 8.7 %all-to-all-start = ((bf16[32,384,128]{2,1,0:T(8,128)(2,1)}), bf16[32,384,128]{2,1,0:T(8,128)(2,1)S(1)}, u32[]{:S(2)}, u32[]{:S(2)}) async-start(bf16[32,384,128]{2,1,0:T(8,128)(2,1)} %bitcast.32), calls=%async_computation | async-start | bytes 6291456 | tf_op jit(solution)/shard_map/all_to_all | solution.py:317
  24.1 0.6 fusion.5
  24.7 0.6 broadcast_in_dim.68
  25.3 1.7 collective-permute-start
  27.0 3.0 %collective-permute-start.1 = (f32[1,128]{1,0:T(1,128)S(1)}, f32[1,128]{1,0:T(1,128)S(1)}, u32[]{:S(2)}, u32[]{:S(2)}) collective-permute-start(f32[1,128]{1,0:T(1,128)S(1)} %broadcast_in_dim.68), channel_id=1, source_target_pairs={{0,64},{32,96},{64,128},{96,160},{128,192},{160,224},{192,0},{224,... | collective-permute-start | bytes 1544 | tf_op jit(solution)/shard_map/ppermute | solution.py:273
  30.0 3.8 %collective-permute-start.2 = (f32[1,128]{1,0:T(1,128)S(1)}, f32[1,128]{1,0:T(1,128)S(1)}, u32[]{:S(2)}, u32[]{:S(2)}) collective-permute-start(f32[1,128]{1,0:T(1,128)S(1)} %broadcast_in_dim.68), channel_id=1, source_target_pairs={{0,96},{32,128},{64,160},{96,192},{128,224},{160,0},{192,32},{224,... | collective-permute-start | bytes 1544 | tf_op jit(solution)/shard_map/ppermute | solution.py:273
  33.8 0.5 collective-permute-start.3
  34.2 4.5 %collective-permute-start.4 = (f32[1,128]{1,0:T(1,128)S(1)}, f32[1,128]{1,0:T(1,128)S(1)}, u32[]{:S(2)}, u32[]{:S(2)}) collective-permute-start(f32[1,128]{1,0:T(1,128)S(1)} %broadcast_in_dim.68), channel_id=1, source_target_pairs={{0,160},{32,192},{64,224},{96,0},{128,32},{160,64},{192,96},{224,1... | collective-permute-start | bytes 1544 | tf_op jit(solution)/shard_map/ppermute | solution.py:273
  38.7 0.0 collective-permute-done
  38.7 2.5 %collective-permute-start.5 = (f32[1,128]{1,0:T(1,128)S(1)}, f32[1,128]{1,0:T(1,128)S(1)}, u32[]{:S(2)}, u32[]{:S(2)}) collective-permute-start(f32[1,128]{1,0:T(1,128)S(1)} %broadcast_in_dim.68), channel_id=1, source_target_pairs={{0,192},{32,224},{64,0},{96,32},{128,64},{160,96},{192,128},{224,1... | collective-permute-start | bytes 1544 | tf_op jit(solution)/shard_map/ppermute | solution.py:273
  41.2 0.0 collective-permute-done.1
  41.2 0.7 collective-permute-start.6
  41.9 0.1 dynamic_slice.3
  42.0 0.0 collective-permute-done.2
  42.0 0.0 collective-permute-done.3
  42.0 0.0 collective-permute-done.4
  42.0 0.5 collective-permute-done.5
  42.5 1.5 collective-permute-done.6
  44.0 0.1 slice_reduce_fusion
  44.1 0.1 select_reduce_fusion.2
  44.2 0.6 pad_add_fusion.slot_ref
  44.8 17.2 %all-to-all-done = bf16[32,384,128]{2,1,0:T(8,128)(2,1)S(1)} async-done(((bf16[32,384,128]{2,1,0:T(8,128)(2,1)}), bf16[32,384,128]{2,1,0:T(8,128)(2,1)S(1)}, u32[]{:S(2)}, u32[]{:S(2)}) %all-to-all-start) | async-done | bytes 3145760 | tf_op jit(solution)/shard_map/all_to_all | solution.py:317
  62.0 7.1 %all-gather.3.cloned.1.call-done = bf16[2048,1024]{1,0:T(8,128)(2,1)} async-done(((bf16[256,1024]{1,0:T(8,128)(2,1)}), bf16[2048,1024]{1,0:T(8,128)(2,1)}) %all-gather.3.cloned.1.call-update) | async-done | bytes 4194320 | tf_op jit(solution)/shard_map/all_gather | solution.py:268
  69.1 7.7 %stats0.1 = f32[8,8,1024]{2,1,0:T(8,128)} custom-call(s32[33]{0:T(128)} %pad_add_fusion.slot_ref, bf16[8,256,1024]{2,1,0:T(8,128)(2,1)} %bitcast.26, bf16[32,2,24,8,128]{4,3,2,1,0:T(8,128)(2,1)} %bitcast.21), custom_call_target="tpu_custom_call" | custom-call | tf_op jit(solution)/shard_map/stats0/pallas_call | solution.py:341
  76.8 4.0 %all-to-all-start.2 = ((f32[8,8,1024]{2,1,0:T(8,128)}), f32[8,8,1024]{2,1,0:T(8,128)S(1)}, u32[]{:S(2)}, u32[]{:S(2)}) async-start(f32[8,8,1024]{2,1,0:T(8,128)} %stats0.1), calls=%async_computation.2 | async-start | bytes 524288 | tf_op jit(solution)/shard_map/all_to_all | solution.py:354
  80.8 7.7 %stats1.1 = f32[8,8,1024]{2,1,0:T(8,128)} custom-call(s32[33]{0:T(128)} %pad_add_fusion.slot_ref, bf16[8,256,1024]{2,1,0:T(8,128)(2,1)} %bitcast.27, bf16[32,2,24,8,128]{4,3,2,1,0:T(8,128)(2,1)} %bitcast.22), custom_call_target="tpu_custom_call" | custom-call | tf_op jit(solution)/shard_map/stats1/pallas_call | solution.py:341
  88.5 2.7 %all-to-all-done.2.stat_ref = f32[8,8,1024]{2,1,0:T(8,128)S(1)} async-done(((f32[8,8,1024]{2,1,0:T(8,128)}), f32[8,8,1024]{2,1,0:T(8,128)S(1)}, u32[]{:S(2)}, u32[]{:S(2)}) %all-to-all-start.2) | async-done | bytes 262176 | tf_op jit(solution)/shard_map/all_to_all | solution.py:354
  91.2 3.9 %all-to-all-start.1 = ((f32[8,8,1024]{2,1,0:T(8,128)}), f32[8,8,1024]{2,1,0:T(8,128)S(1)}, u32[]{:S(2)}, u32[]{:S(2)}) async-start(f32[8,8,1024]{2,1,0:T(8,128)} %stats1.1), calls=%async_computation.1 | async-start | bytes 524288 | tf_op jit(solution)/shard_map/all_to_all | solution.py:354
  95.1 0.2 reduce-scatter.2.cloned.1.call-start
  95.3 11.8 %grads00.1 = (bf16[8,2,128,1024]{3,2,1,0:T(8,128)(2,1)}, bf16[32,2,24,8,128]{4,3,2,1,0:T(8,128)(2,1)}) custom-call(s32[33]{0:T(128)} %pad_add_fusion.slot_ref, bf16[8,256,1024]{2,1,0:T(8,128)(2,1)} %bitcast.28, bf16[32,2,24,8,128]{4,3,2,1,0:T(8,128)(2,1)} %bitcast.23, f32[8,8,1024]{2,1,0:T(8,128)} %copy-done.2), custom_call_target="tpu_custom_call" | custom-call | tf_op jit(solution)/shard_map/grads00/pallas_call | solution.py:367
  107.2 0.7 copy-done.1
  107.9 11.1 %grads10.1 = (bf16[8,2,128,1024]{3,2,1,0:T(8,128)(2,1)}, bf16[32,2,24,8,128]{4,3,2,1,0:T(8,128)(2,1)}) custom-call(s32[33]{0:T(128)} %pad_add_fusion.slot_ref, bf16[8,256,1024]{2,1,0:T(8,128)(2,1)} %bitcast.29, bf16[32,2,24,8,128]{4,3,2,1,0:T(8,128)(2,1)} %bitcast.24, f32[8,8,1024]{2,1,0:T(8,128)} %copy-done.1, ...), custom_call_target="tpu_custom_call", output_to_operand_aliasing={{0}: (4, {}), {1}: (5, {})} | custom-call | tf_op jit(solution)/shard_map/grads10/pallas_call | solution.py:367
  119.0 0.0 reduce-scatter.2.cloned.1.call-update
  119.0 6.1 %grads12.1 = bf16[32,2,24,8,128]{4,3,2,1,0:T(8,128)(2,1)} custom-call(s32[33]{0:T(128)} %pad_add_fusion.slot_ref, bf16[8,256,1024]{2,1,0:T(8,128)(2,1)} %bitcast.30, bf16[32,2,24,8,128]{4,3,2,1,0:T(8,128)(2,1)} %bitcast.25, f32[8,8,1024]{2,1,0:T(8,128)} %copy-done.1, ...), custom_call_target="tpu_custom_call", output_to_operand_aliasing={{}: (4, {})} | custom-call | tf_op jit(solution)/shard_map/grads12/pallas_call | solution.py:367
  125.2 8.8 %all-to-all-start.3 = ((bf16[32,384,128]{2,1,0:T(8,128)(2,1)}), bf16[32,384,128]{2,1,0:T(8,128)(2,1)S(1)}, u32[]{:S(2)}, u32[]{:S(2)}) async-start(bf16[32,384,128]{2,1,0:T(8,128)(2,1)} %bitcast.31), calls=%async_computation.4 | async-start | bytes 6291456 | tf_op jit(solution)/shard_map/all_to_all | solution.py:393
  134.0 0.1 copy.20.spot_ref
  134.1 37.8 %all-to-all-done.3 = bf16[32,384,128]{2,1,0:T(8,128)(2,1)S(1)} async-done(((bf16[32,384,128]{2,1,0:T(8,128)(2,1)}), bf16[32,384,128]{2,1,0:T(8,128)(2,1)S(1)}, u32[]{:S(2)}, u32[]{:S(2)}) %all-to-all-start.3) | async-done | bytes 3145760 | tf_op jit(solution)/shard_map/all_to_all | solution.py:393
  171.9 3.2 %give_back.1 = (bf16[1120,512]{1,0:T(8,128)(2,1)}, bf16[1120,512]{1,0:T(8,128)(2,1)}) custom-call(s32[160,1]{1,0:T(8,128)S(1)} %copy.20.spot_ref, bf16[8,4,2,192,128]{4,3,2,1,0:T(8,128)(2,1)S(1)} %bitcast.20), custom_call_target="tpu_custom_call" | custom-call | tf_op jit(solution)/shard_map/give_back/pallas_call | solution.py:397
  175.2 1.8 reduce-scatter.2.cloned.1.call-done.rows_ref
  177.0 2.0 %turn.1 = (bf16[128,1024]{1,0:T(8,128)(2,1)}, bf16[128,1024]{1,0:T(8,128)(2,1)}) custom-call(bf16[1,2,128,1024]{3,2,1,0:T(8,128)(2,1)} %reduce-scatter.2.cloned.1.call-done.rows_ref), custom_call_target="tpu_custom_call" | custom-call | tf_op jit(solution)/shard_map/turn/pallas_call | solution.py:412
  (14 shorter events, 0.1 us)
Async XLA Ops:
  7.2 61.9 %all-gather.3.cloned.1.call-start = ((), (), s32[]{:S(2)}) async-start(), calls=%async_computation.6 | async-start | bytes 4718592 | tf_op jit(solution)/shard_map/all_gather | solution.py:268
  15.3 8.7 %copy-start.3 = (s32[1,128]{1,0:T(1,128)S(1)}, s32[1,128]{1,0:T(1,128)}, u32[]{:S(2)}) copy-start(s32[1,128]{1,0:T(1,128)} %param.11) | copy-start | bytes 1540
  15.3 46.7 %all-to-all-start = ((bf16[32,384,128]{2,1,0:T(8,128)(2,1)}), bf16[32,384,128]{2,1,0:T(8,128)(2,1)S(1)}, u32[]{:S(2)}, u32[]{:S(2)}) async-start(bf16[32,384,128]{2,1,0:T(8,128)(2,1)} %bitcast.32), calls=%async_computation | async-start | bytes 6291456 | tf_op jit(solution)/shard_map/all_to_all | solution.py:317
  25.3 13.4 %collective-permute-start = (f32[1,128]{1,0:T(1,128)S(1)}, f32[1,128]{1,0:T(1,128)S(1)}, u32[]{:S(2)}, u32[]{:S(2)}) collective-permute-start(f32[1,128]{1,0:T(1,128)S(1)} %broadcast_in_dim.68), channel_id=1, source_target_pairs={{0,32},{32,64},{64,96},{96,128},{128,160},{160,192},{192,224},{224... | collective-permute-start | bytes 1544 | tf_op jit(solution)/shard_map/ppermute | solution.py:273
  27.0 14.2 %collective-permute-start.1 = (f32[1,128]{1,0:T(1,128)S(1)}, f32[1,128]{1,0:T(1,128)S(1)}, u32[]{:S(2)}, u32[]{:S(2)}) collective-permute-start(f32[1,128]{1,0:T(1,128)S(1)} %broadcast_in_dim.68), channel_id=1, source_target_pairs={{0,64},{32,96},{64,128},{96,160},{128,192},{160,224},{192,0},{224,... | collective-permute-start | bytes 1544 | tf_op jit(solution)/shard_map/ppermute | solution.py:273
  30.0 12.0 %collective-permute-start.2 = (f32[1,128]{1,0:T(1,128)S(1)}, f32[1,128]{1,0:T(1,128)S(1)}, u32[]{:S(2)}, u32[]{:S(2)}) collective-permute-start(f32[1,128]{1,0:T(1,128)S(1)} %broadcast_in_dim.68), channel_id=1, source_target_pairs={{0,96},{32,128},{64,160},{96,192},{128,224},{160,0},{192,32},{224,... | collective-permute-start | bytes 1544 | tf_op jit(solution)/shard_map/ppermute | solution.py:273
  33.8 8.2 %collective-permute-start.3 = (f32[1,128]{1,0:T(1,128)S(1)}, f32[1,128]{1,0:T(1,128)S(1)}, u32[]{:S(2)}, u32[]{:S(2)}) collective-permute-start(f32[1,128]{1,0:T(1,128)S(1)} %broadcast_in_dim.68), channel_id=1, source_target_pairs={{0,128},{32,160},{64,192},{96,224},{128,0},{160,32},{192,64},{224,... | collective-permute-start | bytes 1544 | tf_op jit(solution)/shard_map/ppermute | solution.py:273
  34.2 7.8 %collective-permute-start.4 = (f32[1,128]{1,0:T(1,128)S(1)}, f32[1,128]{1,0:T(1,128)S(1)}, u32[]{:S(2)}, u32[]{:S(2)}) collective-permute-start(f32[1,128]{1,0:T(1,128)S(1)} %broadcast_in_dim.68), channel_id=1, source_target_pairs={{0,160},{32,192},{64,224},{96,0},{128,32},{160,64},{192,96},{224,1... | collective-permute-start | bytes 1544 | tf_op jit(solution)/shard_map/ppermute | solution.py:273
  38.7 3.8 %collective-permute-start.5 = (f32[1,128]{1,0:T(1,128)S(1)}, f32[1,128]{1,0:T(1,128)S(1)}, u32[]{:S(2)}, u32[]{:S(2)}) collective-permute-start(f32[1,128]{1,0:T(1,128)S(1)} %broadcast_in_dim.68), channel_id=1, source_target_pairs={{0,192},{32,224},{64,0},{96,32},{128,64},{160,96},{192,128},{224,1... | collective-permute-start | bytes 1544 | tf_op jit(solution)/shard_map/ppermute | solution.py:273
  41.2 2.8 %collective-permute-start.6 = (f32[1,128]{1,0:T(1,128)S(1)}, f32[1,128]{1,0:T(1,128)S(1)}, u32[]{:S(2)}, u32[]{:S(2)}) collective-permute-start(f32[1,128]{1,0:T(1,128)S(1)} %broadcast_in_dim.68), channel_id=1, source_target_pairs={{0,224},{32,0},{64,32},{96,64},{128,96},{160,128},{192,160},{224,1... | collective-permute-start | bytes 1544 | tf_op jit(solution)/shard_map/ppermute | solution.py:273
  62.0 7.1 %copy-start = (bf16[32,384,128]{2,1,0:T(8,128)(2,1)}, bf16[32,384,128]{2,1,0:T(8,128)(2,1)S(1)}, u32[]{:S(2)}) copy-start(bf16[32,384,128]{2,1,0:T(8,128)(2,1)S(1)} %all-to-all-done) | copy-start | bytes 9437188
  76.8 14.4 %all-to-all-start.2 = ((f32[8,8,1024]{2,1,0:T(8,128)}), f32[8,8,1024]{2,1,0:T(8,128)S(1)}, u32[]{:S(2)}, u32[]{:S(2)}) async-start(f32[8,8,1024]{2,1,0:T(8,128)} %stats0.1), calls=%async_computation.2 | async-start | bytes 524288 | tf_op jit(solution)/shard_map/all_to_all | solution.py:354
  91.2 4.2 %copy-start.2 = (f32[8,8,1024]{2,1,0:T(8,128)}, f32[8,8,1024]{2,1,0:T(8,128)S(1)}, u32[]{:S(2)}) copy-start(f32[8,8,1024]{2,1,0:T(8,128)S(1)} %all-to-all-done.2.stat_ref) | copy-start | bytes 786436
  91.2 16.0 %all-to-all-start.1 = ((f32[8,8,1024]{2,1,0:T(8,128)}), f32[8,8,1024]{2,1,0:T(8,128)S(1)}, u32[]{:S(2)}, u32[]{:S(2)}) async-start(f32[8,8,1024]{2,1,0:T(8,128)} %stats1.1), calls=%async_computation.1 | async-start | bytes 524288 | tf_op jit(solution)/shard_map/all_to_all | solution.py:354
  95.1 81.9 %reduce-scatter.2.cloned.1.call-start = ((), (), s32[]{:S(2)}) async-start(), calls=%async_computation.5 | async-start | bytes 4718592 | tf_op jit(solution)/shard_map/reduce_scatter | solution.py:392
  107.2 0.7 copy-start.1
  125.2 46.8 %all-to-all-start.3 = ((bf16[32,384,128]{2,1,0:T(8,128)(2,1)}), bf16[32,384,128]{2,1,0:T(8,128)(2,1)S(1)}, u32[]{:S(2)}, u32[]{:S(2)}) async-start(bf16[32,384,128]{2,1,0:T(8,128)(2,1)} %bitcast.31), calls=%async_computation.4 | async-start | bytes 6291456 | tf_op jit(solution)/shard_map/all_to_all | solution.py:393
Sparse Core Ops, SparseCore 0:
  10.4 58.6 all-gather.2
  119.1 57.7 reduce-scatter.1
